TPU v7x, 256 devices: a whole 4x4x8 slice. The times are simulated.
256 devices in a mesh: seq: 128 (over z, x, y), head: 2 (over core).
Axes of the slice: x: 4, y: 4, z: 8, core: 2. Of those that a mesh axis runs over, the one named last changes fastest.
Arguments:
- queries: bfloat16 [16384, 2048], P(('seq', 'head')), may hold values from -5 to 5
- new_keys: bfloat16 [16384, 2048], P(('seq', 'head')), may hold values from -5 to 5
- new_values: bfloat16 [16384, 2048], P(('seq', 'head')), may hold values from -12 to 12
- grad_out: bfloat16 [16384, 2048], P(('seq', 'head')), may hold values from -192 to 192
- cache_keys: bfloat16 [65536, 2048], P('seq', 'head'), may hold values from -6 to 6
- cache_values: bfloat16 [65536, 2048], P('seq', 'head'), may hold values from -12 to 12
- choices: int32 [2048, 3], P('seq'), may hold values from 0 to 127, as said below
Outputs:
- grad_queries: bfloat16 [16384, 2048], P('seq', 'head')
- grad_new_keys: bfloat16 [16384, 2048], P('seq', 'head')
- grad_new_values: bfloat16 [16384, 2048], P('seq', 'head')
- grad_cache_keys: bfloat16 [65536, 2048], P('seq', 'head')
- grad_cache_values: bfloat16 [65536, 2048], P('seq', 'head')
Inputs may be any that keep to these rules, and one draw needn't show every extreme that they name: `choices`: each row names 3 different blocks. Among the spans of one block of new tokens no cached block is named more than 1 times, and some cached block exactly 1 times.
All inputs are finite; a program needn't handle non-finite values.
Results may differ from a plain program's by a relative error of at most 0.007.
Values may be sent and summed in bfloat16 or wider, within the bound.
A program may use at most 64 MiB of HBM per device.

v0:
```python
import math

import jax
import jax.numpy as jnp
from jax import lax
from jax.sharding import PartitionSpec as P

DH = 128
SPAN = 8
TOPK = 3


def block_stats(query_tile, grad_tile, key_rows, value_rows, scaling, causal_mask):
    scores = (
        jnp.einsum("rhd,khd->hrk", query_tile, key_rows, preferred_element_type=jnp.float32)
        * scaling
    )
    if causal_mask is not None:
        scores = jnp.where(causal_mask[None], scores, -jnp.inf)
    highest = jnp.max(scores, axis=2)
    weights = jnp.exp(scores - highest[:, :, None])
    totals = jnp.sum(weights, axis=2)
    grad_weights = jnp.einsum(
        "rhd,khd->hrk", grad_tile, value_rows, preferred_element_type=jnp.float32
    )
    inners = jnp.sum(weights * grad_weights, axis=2)
    return (highest.T, totals.T, inners.T)


def block_grads(
    query_tile, grad_tile, key_rows, value_rows, log_norm, deltas, scaling, causal_mask
):
    scores = (
        jnp.einsum("rhd,khd->hrk", query_tile, key_rows, preferred_element_type=jnp.float32)
        * scaling
    )
    if causal_mask is not None:
        scores = jnp.where(causal_mask[None], scores, -jnp.inf)
    weights = jnp.exp(scores - log_norm.T[:, :, None])
    grad_weights = jnp.einsum(
        "rhd,khd->hrk", grad_tile, value_rows, preferred_element_type=jnp.float32
    )
    grad_scores = weights * (grad_weights - deltas.T[:, :, None])
    weights_low = weights.astype(jnp.bfloat16)
    grad_low = grad_scores.astype(jnp.bfloat16)
    grad_query = (
        jnp.einsum("hrk,khd->rhd", grad_low, key_rows, preferred_element_type=jnp.float32) * scaling
    )
    grad_keys = (
        jnp.einsum("hrk,rhd->khd", grad_low, query_tile, preferred_element_type=jnp.float32)
        * scaling
    )
    grad_values = jnp.einsum(
        "hrk,rhd->khd", weights_low, grad_tile, preferred_element_type=jnp.float32
    )
    return (grad_query, grad_keys, grad_values)


def body(queries, new_keys, new_values, grad_out, cache_keys, cache_values, choices):
    devices = lax.axis_size("seq")
    query_rows, grad_rows, own_keys, own_values = (
        lax.all_to_all(queries, "head", split_axis=1, concat_axis=0, tiled=True),
        lax.all_to_all(grad_out, "head", split_axis=1, concat_axis=0, tiled=True),
        lax.all_to_all(new_keys, "head", split_axis=1, concat_axis=0, tiled=True),
        lax.all_to_all(new_values, "head", split_axis=1, concat_axis=0, tiled=True),
    )
    local_feats = cache_keys.shape[1]
    local_heads = local_feats // DH
    block_len = cache_keys.shape[0]
    span_count = choices.shape[0]
    rows_here = query_rows.shape[0]
    scaling = 1.0 / math.sqrt(DH)
    capacity = -(-(TOPK * span_count) // devices)
    slot_total = devices * capacity
    row_total = slot_total * SPAN
    flat_picks = choices.reshape(-1)
    pick_count = flat_picks.shape[0]
    owner_hits = (flat_picks[:, None] == jnp.arange(devices, dtype=jnp.int32)[None, :]).astype(
        jnp.int32
    )
    earlier = jnp.cumsum(owner_hits, axis=0) - owner_hits
    rank_at = jnp.sum(earlier * owner_hits, axis=1)
    slot_of_pick = flat_picks * capacity + rank_at
    slot_hits = (slot_of_pick[:, None] == jnp.arange(slot_total, dtype=jnp.int32)[None, :]).astype(
        jnp.int32
    )
    span_of_pick = jnp.arange(pick_count, dtype=jnp.int32) // TOPK
    source_span = jnp.sum(slot_hits * (span_of_pick[:, None] + 1), axis=0) - 1
    filled = source_span >= 0
    safe_span = jnp.maximum(source_span, 0)

    def to_slots(source):
        picked = jnp.take(source, safe_span, axis=0)
        picked = jnp.where(filled[:, None, None], picked, jnp.zeros_like(picked))
        return picked

    def per_pick(returned, width):
        return jnp.take(returned, slot_of_pick, axis=0).reshape(span_count, TOPK, SPAN, width)

    send_query = to_slots(query_rows.reshape(span_count, SPAN, local_feats))
    send_grad = to_slots(grad_rows.reshape(span_count, SPAN, local_feats))
    recv_query, recv_grad = (
        lax.all_to_all(send_query, "seq", split_axis=0, concat_axis=0, tiled=True),
        lax.all_to_all(send_grad, "seq", split_axis=0, concat_axis=0, tiled=True),
    )
    key_rows = cache_keys.reshape(block_len, local_heads, DH)
    value_rows = cache_values.reshape(block_len, local_heads, DH)
    tile_slots = math.gcd(slot_total, max(1, 512 // SPAN))
    tile_rows = tile_slots * SPAN
    tile_count = slot_total // tile_slots
    ordering = jnp.arange(slot_total, dtype=jnp.int32)
    work_query = recv_query
    work_grad = recv_grad
    work_query = work_query.reshape(row_total, local_heads, DH)
    work_grad = work_grad.reshape(row_total, local_heads, DH)

    def first_pass(tile_index, buffers):
        peaks, totals, inners = buffers
        first_row = tile_index * tile_rows
        tile_query = lax.dynamic_slice_in_dim(work_query, first_row, tile_rows, 0)
        tile_grad = lax.dynamic_slice_in_dim(work_grad, first_row, tile_rows, 0)
        tile_peak, tile_total, tile_inner = block_stats(
            tile_query, tile_grad, key_rows, value_rows, scaling, None
        )
        return (
            lax.dynamic_update_slice_in_dim(peaks, tile_peak, first_row, 0),
            lax.dynamic_update_slice_in_dim(totals, tile_total, first_row, 0),
            lax.dynamic_update_slice_in_dim(inners, tile_inner, first_row, 0),
        )

    empty_stats = jnp.zeros((row_total, local_heads), jnp.float32)
    peaks, totals, inners = lax.fori_loop(
        0, tile_count, first_pass, (empty_stats, empty_stats, empty_stats)
    )
    back_peaks, back_totals, back_inners = (
        lax.all_to_all(
            peaks.reshape(devices, capacity * SPAN, local_heads),
            "seq",
            split_axis=0,
            concat_axis=0,
            tiled=True,
        ),
        lax.all_to_all(
            totals.reshape(devices, capacity * SPAN, local_heads),
            "seq",
            split_axis=0,
            concat_axis=0,
            tiled=True,
        ),
        lax.all_to_all(
            inners.reshape(devices, capacity * SPAN, local_heads),
            "seq",
            split_axis=0,
            concat_axis=0,
            tiled=True,
        ),
    )
    places = jnp.arange(rows_here, dtype=jnp.int32)
    causal = places[None, :] <= places[:, None]
    own_query = query_rows.reshape(rows_here, local_heads, DH)
    own_grad = grad_rows.reshape(rows_here, local_heads, DH)
    own_key_rows = own_keys.reshape(rows_here, local_heads, DH)
    own_value_rows = own_values.reshape(rows_here, local_heads, DH)
    own_peak, own_total, own_inner = block_stats(
        own_query, own_grad, own_key_rows, own_value_rows, scaling, causal
    )
    own_peak = own_peak.reshape(span_count, SPAN, local_heads)
    own_total = own_total.reshape(span_count, SPAN, local_heads)
    own_inner = own_inner.reshape(span_count, SPAN, local_heads)
    pick_peak = per_pick(back_peaks, local_heads)
    pick_total = per_pick(back_totals, local_heads)
    pick_inner = per_pick(back_inners, local_heads)
    joint_peak = jnp.maximum(own_peak, jnp.max(pick_peak, axis=1))
    joint_total = own_total * jnp.exp(own_peak - joint_peak) + jnp.sum(
        pick_total * jnp.exp(pick_peak - joint_peak[:, None]), axis=1
    )
    log_norm = joint_peak + jnp.log(joint_total)
    deltas = own_inner * jnp.exp(own_peak - log_norm) + jnp.sum(
        pick_inner * jnp.exp(pick_peak - log_norm[:, None]), axis=1
    )
    out_norm, out_delta = (
        lax.all_to_all(to_slots(log_norm), "seq", split_axis=0, concat_axis=0, tiled=True),
        lax.all_to_all(to_slots(deltas), "seq", split_axis=0, concat_axis=0, tiled=True),
    )
    work_norm = jnp.take(out_norm, ordering, axis=0).reshape(row_total, local_heads)
    work_delta = jnp.take(out_delta, ordering, axis=0).reshape(row_total, local_heads)

    def second_pass(tile_index, carried):
        sum_keys, sum_values, grad_slots = carried
        first_row = tile_index * tile_rows
        tile_query = lax.dynamic_slice_in_dim(work_query, first_row, tile_rows, 0)
        tile_grad = lax.dynamic_slice_in_dim(work_grad, first_row, tile_rows, 0)
        tile_norm = lax.dynamic_slice_in_dim(work_norm, first_row, tile_rows, 0)
        tile_delta = lax.dynamic_slice_in_dim(work_delta, first_row, tile_rows, 0)
        grad_query, grad_keys, grad_values = block_grads(
            tile_query, tile_grad, key_rows, value_rows, tile_norm, tile_delta, scaling, None
        )
        return (
            sum_keys + grad_keys,
            sum_values + grad_values,
            lax.dynamic_update_slice_in_dim(
                grad_slots, grad_query.astype(jnp.bfloat16), first_row, 0
            ),
        )

    zero_block = jnp.zeros((block_len, local_heads, DH), jnp.float32)
    zero_slots = jnp.zeros((row_total, local_heads, DH), jnp.bfloat16)
    sum_keys, sum_values, grad_slots = lax.fori_loop(
        0, tile_count, second_pass, (zero_block, zero_block, zero_slots)
    )
    back_grads = lax.all_to_all(
        grad_slots.reshape(devices, capacity * SPAN, local_feats),
        "seq",
        split_axis=0,
        concat_axis=0,
        tiled=True,
    )
    own_gq, own_gk, own_gv = block_grads(
        own_query,
        own_grad,
        own_key_rows,
        own_value_rows,
        log_norm.reshape(rows_here, local_heads),
        deltas.reshape(rows_here, local_heads),
        scaling,
        causal,
    )
    pick_grads = jnp.sum(per_pick(back_grads, local_feats).astype(jnp.float32), axis=1).reshape(
        rows_here, local_feats
    )
    grad_queries = (own_gq.reshape(rows_here, local_feats) + pick_grads).astype(jnp.bfloat16)
    grad_new_keys = own_gk.reshape(rows_here, local_feats).astype(jnp.bfloat16)
    grad_new_values = own_gv.reshape(rows_here, local_feats).astype(jnp.bfloat16)
    grad_cache_keys = sum_keys.reshape(block_len, local_feats).astype(jnp.bfloat16)
    grad_cache_values = sum_values.reshape(block_len, local_feats).astype(jnp.bfloat16)
    return (grad_queries, grad_new_keys, grad_new_values, grad_cache_keys, grad_cache_values)


def solution(mesh):
    return jax.shard_map(
        body,
        mesh=mesh,
        in_specs=(
            P(("seq", "head"), None),
            P(("seq", "head"), None),
            P(("seq", "head"), None),
            P(("seq", "head"), None),
            P("seq", "head"),
            P("seq", "head"),
            P("seq", None),
        ),
        out_specs=(
            P("seq", "head"),
            P("seq", "head"),
            P("seq", "head"),
            P("seq", "head"),
            P("seq", "head"),
        ),
        check_vma=False,
    )
```

profile of v0, /device:TPU:32, one launch (start us, length us, event | category | flops | bytes accessed | tf_op | source)
XLA Modules:
  0.0 405.5 jit_solution(16904331700355983113)
XLA Ops:
  0.6 1.7 copy.316
  2.4 3.4 all-to-all-start.3
  10.6 3.5 all-to-all-start
  15.6 3.4 all-to-all-start.1
  19.0 2.0 gather_fusion.1
  21.1 3.7 select_select_fusion
  24.8 3.9 all_to_all.104
  28.7 68.8 %all_to_all.105 = bf16[128,8,1024]{2,1,0:T(8,128)(2,1)} all-to-all(bf16[128,8,1024]{2,1,0:T(8,128)(2,1)} %get-tuple-element.530), channel_id=1, replica_groups=mesh['seq'=128,'head'=2] {'seq'}, dimensions={0} | all-to-all | bytes 4194304 | tf_op jit(solution)/shard_map/all_to_all | solution.py:104
  97.5 6.9 %all-to-all-start.2 = ((bf16[128,8,1024]{2,1,0:T(8,128)(2,1)}), bf16[128,8,1024]{2,1,0:T(8,128)(2,1)S(1)}, u32[]{:S(2)}, u32[]{:S(2)}) async-start(bf16[128,8,1024]{2,1,0:T(8,128)(2,1)} %get-tuple-element.531), calls=%async_computation.2 | async-start | bytes 4194304 | tf_op jit(solution)/shard_map/all_to_all | solution.py:103
  109.0 2.3 copy.231
  112.9 2.3 copy.233
  115.2 2.3 copy.237
  117.5 2.0 fusion.37
  119.5 2.2 copy.303
  123.4 33.8 %all-to-all-done.2 = bf16[128,8,1024]{2,1,0:T(8,128)(2,1)S(1)} async-done(((bf16[128,8,1024]{2,1,0:T(8,128)(2,1)}), bf16[128,8,1024]{2,1,0:T(8,128)(2,1)S(1)}, u32[]{:S(2)}, u32[]{:S(2)}) %all-to-all-start.2) | async-done | bytes 2097184 | tf_op jit(solution)/shard_map/all_to_all | solution.py:103
  158.1 10.2 %while.35 = (s32[]{:T(128)}, f32[1024,8]{0,1:T(8,128)S(1)}, f32[1024,8]{0,1:T(8,128)S(1)}, f32[1024,8]{0,1:T(8,128)S(1)}, bf16[1024,8,128]{2,0,1:T(8,128)(2,1)S(...) while((s32[]{:T(128)}, f32[1024,8]{0,1:T(8,128)S(1)}, ...), condition=%wide.region_8.10_spmd, body=%wide.region_4.9_spmd.sunk | while | flops 1092603904 | bytes 42123500 | solution.py:132
  161.3 1.9 multiply_reduce_fusion.8
  166.4 1.9 multiply_reduce_fusion.8
  169.4 6.9 %all-to-all-start.8 = ((f32[128,8,8]{2,1,0:T(8,128)}), f32[128,8,8]{2,1,0:T(8,128)}, u32[]{:S(2)}, u32[]{:S(2)}) async-start(f32[128,8,8]{2,1,0:T(8,128)} %bitcast.179), calls=%async_computation.8 | async-start | bytes 1048576 | tf_op jit(solution)/shard_map/all_to_all | solution.py:150
  176.2 2.2 multiply_reduce_fusion.2
  179.5 15.7 %all-to-all-done.8 = f32[128,8,8]{2,1,0:T(8,128)} async-done(((f32[128,8,8]{2,1,0:T(8,128)}), f32[128,8,8]{2,1,0:T(8,128)}, u32[]{:S(2)}, u32[]{:S(2)}) %all-to-all-start.8) | async-done | bytes 32800 | tf_op jit(solution)/shard_map/all_to_all | solution.py:150
  195.1 7.7 %all-to-all-start.5 = ((f32[128,8,8]{2,1,0:T(8,128)}), f32[128,8,8]{2,1,0:T(8,128)}, u32[]{:S(2)}, u32[]{:S(2)}) async-start(f32[128,8,8]{2,1,0:T(8,128)} %bitcast.177), calls=%async_computation.5 | async-start | bytes 1048576 | tf_op jit(solution)/shard_map/all_to_all | solution.py:136
  205.7 14.3 %all-to-all-done.5 = f32[128,8,8]{2,1,0:T(8,128)} async-done(((f32[128,8,8]{2,1,0:T(8,128)}), f32[128,8,8]{2,1,0:T(8,128)}, u32[]{:S(2)}, u32[]{:S(2)}) %all-to-all-start.5) | async-done | bytes 32800 | tf_op jit(solution)/shard_map/all_to_all | solution.py:136
  220.0 7.5 %all-to-all-start.6 = ((f32[128,8,8]{2,1,0:T(8,128)}), f32[128,8,8]{2,1,0:T(8,128)}, u32[]{:S(2)}, u32[]{:S(2)}) async-start(f32[128,8,8]{2,1,0:T(8,128)} %bitcast.178), calls=%async_computation.6 | async-start | bytes 1048576 | tf_op jit(solution)/shard_map/all_to_all | solution.py:143
  227.5 2.3 gather_fusion.5
  229.8 2.3 gather_fusion.3
  232.1 10.8 %all-to-all-done.6 = f32[128,8,8]{2,1,0:T(8,128)} async-done(((f32[128,8,8]{2,1,0:T(8,128)}), f32[128,8,8]{2,1,0:T(8,128)}, u32[]{:S(2)}, u32[]{:S(2)}) %all-to-all-start.6) | async-done | bytes 32800 | tf_op jit(solution)/shard_map/all_to_all | solution.py:143
  242.9 2.3 gather_fusion.4
  245.2 2.0 broadcast_select_fusion.1
  251.9 1.7 gather_fusion.6
  258.7 2.5 select_select_fusion.2
  261.2 7.8 %all-to-all-start.10 = ((f32[128,8,8]{2,1,0:T(8,128)}), f32[128,8,8]{2,1,0:T(8,128)}, u32[]{:S(2)}, u32[]{:S(2)}) async-start(f32[128,8,8]{2,1,0:T(8,128)} %get-tuple-element.528), calls=%async_computation.10 | async-start | bytes 1048576 | tf_op jit(solution)/shard_map/all_to_all | solution.py:183
  269.1 15.8 %all-to-all-done.10 = f32[128,8,8]{2,1,0:T(8,128)} async-done(((f32[128,8,8]{2,1,0:T(8,128)}), f32[128,8,8]{2,1,0:T(8,128)}, u32[]{:S(2)}, u32[]{:S(2)}) %all-to-all-start.10) | async-done | bytes 32800 | tf_op jit(solution)/shard_map/all_to_all | solution.py:183
  284.8 7.9 %all-to-all-start.9 = ((f32[128,8,8]{2,1,0:T(8,128)}), f32[128,8,8]{2,1,0:T(8,128)}, u32[]{:S(2)}, u32[]{:S(2)}) async-start(f32[128,8,8]{2,1,0:T(8,128)} %get-tuple-element.529), calls=%async_computation.9 | async-start | bytes 1048576 | tf_op jit(solution)/shard_map/all_to_all | solution.py:182
  292.7 2.5 gather_fusion.9
  295.2 13.1 %all-to-all-done.9 = f32[128,8,8]{2,1,0:T(8,128)} async-done(((f32[128,8,8]{2,1,0:T(8,128)}), f32[128,8,8]{2,1,0:T(8,128)}, u32[]{:S(2)}, u32[]{:S(2)}) %all-to-all-start.9) | async-done | bytes 32800 | tf_op jit(solution)/shard_map/all_to_all | solution.py:182
  308.3 2.5 gather_fusion.7
  310.8 2.5 select_bitcast_fusion
  315.7 1.7 broadcast_in_dim.125.clone
  317.3 26.8 %while.36 = (s32[]{:T(128)}, f32[512,8,128]{0,2,1:T(8,128)}, f32[512,8,128]{0,2,1:T(8,128)}, bf16[1024,8,128]{2,1,0:T(8,128)(2,1)}, bf16[1024,8,128]{2,0,1:T(8,1...) while((s32[]{:T(128)}, f32[512,8,128]{0,2,1:T(8,128)}, ...), condition=%wide.region_15.20_spmd.clone, body=%wide.region_14.19_spmd.clone.sunk | while | flops 2704801792 | bytes 119652800 | solution.py:208
  319.6 2.6 bitcast_add_fusion.7
  322.2 2.6 multiply_convert_fusion.4
  333.0 2.6 bitcast_add_fusion.7
  335.6 2.6 multiply_convert_fusion.4
  344.1 4.2 %reshape.267 = bf16[128,8,1024]{2,1,0:T(8,128)(2,1)} reshape(bf16[1024,8,128]{2,1,0:T(8,128)(2,1)} %get-tuple-element.324) | data formatting | bytes 4194304 | tf_op jit(solution)/shard_map/reshape | solution.py:212
  348.3 7.6 %all-to-all-start.11 = ((bf16[128,8,1024]{2,1,0:T(8,128)(2,1)}), bf16[128,8,1024]{2,1,0:T(8,128)(2,1)}, u32[]{:S(2)}, u32[]{:S(2)}) async-start(bf16[128,8,1024]{2,1,0:T(8,128)(2,1)} %reshape.267), calls=%async_computation.11 | async-start | bytes 4194304 | tf_op jit(solution)/shard_map/all_to_all | solution.py:211
  366.1 35.6 %all-to-all-done.11 = bf16[128,8,1024]{2,1,0:T(8,128)(2,1)} async-done(((bf16[128,8,1024]{2,1,0:T(8,128)(2,1)}), bf16[128,8,1024]{2,1,0:T(8,128)(2,1)}, u32[]{:S(2)}, u32[]{:S(2)}) %all-to-all-start.11) | async-done | bytes 2097184 | tf_op jit(solution)/shard_map/all_to_all | solution.py:211
  401.7 2.3 gather_fusion
  (188 shorter events, 65.5 us)
Async XLA Ops:
  0.6 9.9 %copy-start.23 = (bf16[64,2048]{1,0:T(8,128)(2,1)S(1)}, bf16[64,2048]{1,0:T(8,128)(2,1)}, u32[]{:S(2)}) copy-start(bf16[64,2048]{1,0:T(8,128)(2,1)} %param.21) | copy-start | bytes 786436
  2.4 8.2 %all-to-all-start.3 = ((bf16[64,2,1024]{2,0,1:T(8,128)(2,1)}), bf16[64,2,1024]{2,0,1:T(8,128)(2,1)S(1)}, u32[]{:S(2)}, u32[]{:S(2)}) async-start(bf16[64,2,1024]{2,0,1:T(8,128)(2,1)} %bitcast.132), calls=%async_computation.3 | async-start | bytes 524288 | tf_op jit(solution)/shard_map/all_to_all | solution.py:63
  7.0 7.7 %copy-start.28 = (s32[48]{0:T(128)}, s32[48]{0:T(128)S(1)}, u32[]{:S(2)}) copy-start(s32[48]{0:T(128)S(1)} %select_reduce_fusion.1) | copy-start | bytes 580
  7.2 13.9 %copy-start.30 = (pred[128]{0:T(512)(128)(4,1)}, pred[128]{0:T(512)(128)(4,1)S(1)}, u32[]{:S(2)}) copy-start(pred[128]{0:T(512)(128)(4,1)S(1)} %get-tuple-element.537) | copy-start | bytes 388
  7.2 13.9 %copy-start.31 = (pred[128]{0:T(512)(128)(4,1)}, pred[128]{0:T(512)(128)(4,1)S(1)}, u32[]{:S(2)}) copy-start(pred[128]{0:T(512)(128)(4,1)S(1)} %get-tuple-element.538) | copy-start | bytes 388
  7.2 11.8 %copy-start.26 = (s32[1024]{0:T(1024)}, s32[1024]{0:T(1024)S(1)}, u32[]{:S(2)}) copy-start(s32[1024]{0:T(1024)S(1)} %pad_clamp_fusion.3) | copy-start | bytes 12292
  10.6 5.0 %all-to-all-start = ((bf16[64,2,1024]{2,0,1:T(8,128)(2,1)}), bf16[64,2,1024]{2,0,1:T(8,128)(2,1)S(1)}, u32[]{:S(2)}, u32[]{:S(2)}) async-start(bf16[64,2,1024]{2,0,1:T(8,128)(2,1)} %bitcast.133), calls=%async_computation | async-start | bytes 524288 | tf_op jit(solution)/shard_map/all_to_all | solution.py:62
  15.6 9.2 %all-to-all-start.1 = ((bf16[64,2,1024]{2,0,1:T(8,128)(2,1)}), bf16[64,2,1024]{2,0,1:T(8,128)(2,1)S(1)}, u32[]{:S(2)}, u32[]{:S(2)}) async-start(bf16[64,2,1024]{2,0,1:T(8,128)(2,1)} %bitcast.134), calls=%async_computation.1 | async-start | bytes 524288 | tf_op jit(solution)/shard_map/all_to_all | solution.py:64
  24.8 72.7 %copy-start.19 = (bf16[64,2,1024]{2,0,1:T(8,128)(2,1)}, bf16[64,2,1024]{2,0,1:T(8,128)(2,1)S(1)}, u32[]{:S(2)}) copy-start(bf16[64,2,1024]{2,0,1:T(8,128)(2,1)S(1)} %all-to-all-done.1) | copy-start | bytes 786436
  97.5 8.9 %copy-start.20 = (bf16[64,2,1024]{2,0,1:T(8,128)(2,1)S(1)}, bf16[64,2,1024]{2,0,1:T(8,128)(2,1)}, u32[]{:S(2)}) copy-start(bf16[64,2,1024]{2,0,1:T(8,128)(2,1)} %copy-done.19) | copy-start | bytes 786436
  97.5 59.7 %all-to-all-start.2 = ((bf16[128,8,1024]{2,1,0:T(8,128)(2,1)}), bf16[128,8,1024]{2,1,0:T(8,128)(2,1)S(1)}, u32[]{:S(2)}, u32[]{:S(2)}) async-start(bf16[128,8,1024]{2,1,0:T(8,128)(2,1)} %get-tuple-element.531), calls=%async_computation.2 | async-start | bytes 4194304 | tf_op jit(solution)/shard_map/all_to_all | solution.py:103
  106.3 11.1 %copy-start.13 = (bf16[128,8,128]{0,2,1:T(8,128)(2,1)}, bf16[128,8,128]{0,2,1:T(8,128)(2,1)S(1)}, u32[]{:S(2)}) copy-start(bf16[128,8,128]{0,2,1:T(8,128)(2,1)S(1)} %copy.272) | copy-start | bytes 786436
  158.1 18.1 %copy-start.16 = (bf16[128,8,128]{0,2,1:T(8,128)(2,1)S(1)}, bf16[128,8,128]{0,2,1:T(8,128)(2,1)}, u32[]{:S(2)}) copy-start(bf16[128,8,128]{0,2,1:T(8,128)(2,1)} %copy.274) | copy-start | bytes 786436
  159.4 1.6 copy-start.6
  159.5 1.8 copy-start.8
  164.6 1.6 copy-start.6
  164.6 1.8 copy-start.8
  169.4 25.7 %all-to-all-start.8 = ((f32[128,8,8]{2,1,0:T(8,128)}), f32[128,8,8]{2,1,0:T(8,128)}, u32[]{:S(2)}, u32[]{:S(2)}) async-start(f32[128,8,8]{2,1,0:T(8,128)} %bitcast.179), calls=%async_computation.8 | async-start | bytes 1048576 | tf_op jit(solution)/shard_map/all_to_all | solution.py:150
  178.5 53.7 %copy-start.24 = (f32[8,128]{1,0:T(8,128)}, f32[8,128]{1,0:T(8,128)S(1)}, u32[]{:S(2)}) copy-start(f32[8,128]{1,0:T(8,128)S(1)} %get-tuple-element.481) | copy-start | bytes 12292
  195.1 24.9 %all-to-all-start.5 = ((f32[128,8,8]{2,1,0:T(8,128)}), f32[128,8,8]{2,1,0:T(8,128)}, u32[]{:S(2)}, u32[]{:S(2)}) async-start(f32[128,8,8]{2,1,0:T(8,128)} %bitcast.177), calls=%async_computation.5 | async-start | bytes 1048576 | tf_op jit(solution)/shard_map/all_to_all | solution.py:136
  203.1 46.6 %copy-start.22 = (f32[16,8,8]{0,2,1:T(8,128)}, f32[16,8,8]{0,2,1:T(8,128)S(1)}, u32[]{:S(2)}) copy-start(f32[16,8,8]{0,2,1:T(8,128)S(1)} %copy.241) | copy-start | bytes 12292
  220.0 22.9 %all-to-all-start.6 = ((f32[128,8,8]{2,1,0:T(8,128)}), f32[128,8,8]{2,1,0:T(8,128)}, u32[]{:S(2)}, u32[]{:S(2)}) async-start(f32[128,8,8]{2,1,0:T(8,128)} %bitcast.178), calls=%async_computation.6 | async-start | bytes 1048576 | tf_op jit(solution)/shard_map/all_to_all | solution.py:143
  261.2 23.6 %all-to-all-start.10 = ((f32[128,8,8]{2,1,0:T(8,128)}), f32[128,8,8]{2,1,0:T(8,128)}, u32[]{:S(2)}, u32[]{:S(2)}) async-start(f32[128,8,8]{2,1,0:T(8,128)} %get-tuple-element.528), calls=%async_computation.10 | async-start | bytes 1048576 | tf_op jit(solution)/shard_map/all_to_all | solution.py:183
  284.8 23.5 %all-to-all-start.9 = ((f32[128,8,8]{2,1,0:T(8,128)}), f32[128,8,8]{2,1,0:T(8,128)}, u32[]{:S(2)}, u32[]{:S(2)}) async-start(f32[128,8,8]{2,1,0:T(8,128)} %get-tuple-element.529), calls=%async_computation.9 | async-start | bytes 1048576 | tf_op jit(solution)/shard_map/all_to_all | solution.py:182
  317.3 1.6 copy-start.3
  317.4 2.2 copy-start.7
  319.6 2.6 copy-start.9
  322.2 2.7 copy-start.4
  324.9 1.6 copy-start
  326.4 1.6 copy-start.11
  330.7 1.6 copy-start.3
  330.7 2.2 copy-start.7
  332.9 2.6 copy-start.9
  335.6 2.7 copy-start.4
  338.2 1.6 copy-start
  339.8 1.6 copy-start.11
  348.3 7.8 %copy-start.29 = (s32[48]{0:T(128)S(1)}, s32[48]{0:T(128)}, u32[]{:S(2)}) copy-start(s32[48]{0:T(128)} %copy-done.28) | copy-start | bytes 580
  348.3 9.2 %copy-start.21 = (f32[16,8,8]{2,1,0:T(8,128)S(1)}, f32[16,8,8]{2,1,0:T(8,128)}, u32[]{:S(2)}) copy-start(f32[16,8,8]{2,1,0:T(8,128)} %multiply_reduce_fusion.3) | copy-start | bytes 12292
  348.3 9.2 %copy-start.25 = (f32[8,128]{1,0:T(8,128)S(1)}, f32[8,128]{1,0:T(8,128)}, u32[]{:S(2)}) copy-start(f32[8,128]{1,0:T(8,128)} %copy-done.24) | copy-start | bytes 12292
  348.3 9.3 %copy-start.10 = (f32[8,128,128]{1,2,0:T(8,128)S(1)}, f32[8,128,128]{1,2,0:T(8,128)}, u32[]{:S(2)}) copy-start(f32[8,128,128]{1,2,0:T(8,128)} %get-tuple-element.540) | copy-start | bytes 1572868
  348.3 9.3 %copy-start.17 = (bf16[128,8,128]{0,2,1:T(8,128)(2,1)S(1)}, bf16[128,8,128]{0,2,1:T(8,128)(2,1)}, u32[]{:S(2)}) copy-start(bf16[128,8,128]{0,2,1:T(8,128)(2,1)} %copy.274) | copy-start | bytes 786436
  348.3 53.4 %all-to-all-start.11 = ((bf16[128,8,1024]{2,1,0:T(8,128)(2,1)}), bf16[128,8,1024]{2,1,0:T(8,128)(2,1)}, u32[]{:S(2)}, u32[]{:S(2)}) async-start(bf16[128,8,1024]{2,1,0:T(8,128)(2,1)} %reshape.267), calls=%async_computation.11 | async-start | bytes 4194304 | tf_op jit(solution)/shard_map/all_to_all | solution.py:211
  355.9 4.1 %copy-start.15 = (bf16[128,8,128]{0,2,1:T(8,128)(2,1)S(1)}, bf16[128,8,128]{0,2,1:T(8,128)(2,1)}, u32[]{:S(2)}) copy-start(bf16[128,8,128]{0,2,1:T(8,128)(2,1)} %copy.255) | copy-start | bytes 786436
  357.9 3.5 copy-start.14
  358.8 3.8 copy-start.2
  362.7 2.0 copy-start.5
  364.8 39.3 %copy-start.27 = (pred[16,3]{1,0:T(8,128)(4,1)S(1)}, pred[16,3]{1,0:T(8,128)(4,1)}, u32[]{:S(2)}) copy-start(pred[16,3]{1,0:T(8,128)(4,1)} %compare_and_fusion) | copy-start | bytes 148
  364.8 39.5 %copy-start.18 = (f32[128,1024]{1,0:T(8,128)S(1)}, f32[128,1024]{1,0:T(8,128)}, u32[]{:S(2)}) copy-start(f32[128,1024]{1,0:T(8,128)} %copy.270) | copy-start | bytes 1572868
  (4 other events, 5.4 us)
where the time goes:
time: 412 us; the launch traced here: 406 us
  waiting for transfers between devices  140 us (34%)
  local copies, waits for them, and re-layouts  76 us (18%)
  blocking collectives  72.7 us (18%)
  starting transfers between devices  62.7 us (15%)
  matrix products  29.6 us (7%)
  other arithmetic  22.6 us (5%)
    all_to_all x1, blocking collectives, body(): lax.all_to_all(send_grad, 'seq', split_axis=0, concat_axis=0, tiled=True)  68.8 us
    all_to_all x1, waiting for transfers between devices, body(): lax.all_to_all(grad_slots.reshape(devices, capacity * SPAN, local_feats),...  35.6 us
    all_to_all x1, waiting for transfers between devices, body(): lax.all_to_all(send_query, 'seq', split_axis=0, concat_axis=0, tiled=True)  33.8 us
    all_to_all x1, waiting for transfers between devices, body(): lax.all_to_all(to_slots(deltas), 'seq', split_axis=0, concat_axis=0, tile...  15.8 us
    all_to_all x1, waiting for transfers between devices, body(): lax.all_to_all(inners.reshape(devices, capacity * SPAN, local_heads), 'se...  15.7 us
    all_to_all x1, waiting for transfers between devices, body(): lax.all_to_all(peaks.reshape(devices, capacity * SPAN, local_heads), 'seq...  14.3 us
    all_to_all x1, waiting for transfers between devices, body(): lax.all_to_all(to_slots(log_norm), 'seq', split_axis=0, concat_axis=0, ti...  13.1 us
    unnamed x55, local copies, waits for them, and re-layouts  12.2 us
  transfers between devices with their start and end apart: 10, of which 8 were waited for; matrix products, arithmetic and copies ran while one was open for 13% of the time, Pallas kernels for 0%

commit v1 on v0

v1 whole, which is shorter than its diff:
```python
import functools
import math

import jax
import jax.numpy as jnp
from jax import lax
from jax.experimental import pallas as pl
from jax.experimental.pallas import tpu as pltpu
from jax.sharding import PartitionSpec as P

DH = 128
SPAN = 8
TOPK = 3
NZ = 8
NX = 4
NY = 4
PLANE = NX * NY
SPANS = 16
FEATS = 1024
HEADS = FEATS // DH
ROWS = SPANS * SPAN
MESH = pl.DeviceIdType.MESH
OFFSETS = (0, -1, 1, -2, 2, -3, 3, 4)
GROUP_OF = (0, 2, 4, 6, 7, 5, 3, 1)


def dispatch_kernel(
    q_ref, g_ref, k_ref, v_ref, tab_ref,
    rbuf, qrows, grows, krows, vrows,
    zbufs, sbuf, tabz, tab_smem,
    head_send, head_recv, local_sem, tab_send, tab_recv, ring_send, ring_recv,
    plane_send, plane_recv,
):
    seq = lax.axis_index("seq")
    head = lax.axis_index("head")
    z = seq // PLANE
    t0 = seq % PLANE
    x0 = t0 // NY
    y0 = t0 % NY

    def z_peer(d):
        return (((z + d) % NZ) * PLANE + t0, head)

    def plane_of(o):
        return ((x0 + o // NY) % NX) * NY + (y0 + o % NY) % NY

    sibling = (seq, 1 - head)
    barrier = pltpu.get_barrier_semaphore()
    pl.semaphore_signal(barrier, inc=1, device_id=sibling, device_id_type=MESH)
    for d in range(1, NZ):
        pl.semaphore_signal(barrier, inc=1, device_id=z_peer(d), device_id_type=MESH)

    def greet(o, carry):
        pl.semaphore_signal(
            barrier, inc=1, device_id=(z * PLANE + plane_of(o), head), device_id_type=MESH
        )
        return carry

    lax.fori_loop(1, PLANE, greet, 0)
    pl.semaphore_wait(barrier, 1 + (NZ - 1) + (PLANE - 1))

    half = ROWS // 2
    my_rows = pl.ds(pl.multiple_of(head * half, half), half)
    my_cols = pl.ds(pl.multiple_of(head * FEATS, FEATS), FEATS)
    other_cols = pl.ds(pl.multiple_of((1 - head) * FEATS, FEATS), FEATS)
    swaps, locals_ = [], []
    for i, (src, dst) in enumerate(
        ((q_ref, qrows), (g_ref, grows), (k_ref, krows), (v_ref, vrows))
    ):
        swap = pltpu.make_async_remote_copy(
            src_ref=src.at[:, other_cols], dst_ref=dst.at[my_rows, :],
            send_sem=head_send.at[i], recv_sem=head_recv.at[i],
            device_id=sibling, device_id_type=MESH,
        )
        swap.start()
        swaps.append(swap)
        keep = pltpu.make_async_copy(src.at[:, my_cols], dst.at[my_rows, :], local_sem.at[i])
        keep.start()
        locals_.append(keep)
    tabs = []
    for d in range(1, NZ):
        tab = pltpu.make_async_remote_copy(
            src_ref=tab_ref.at[(z + d) % NZ], dst_ref=tabz.at[GROUP_OF[(-d) % NZ]],
            send_sem=tab_send.at[d], recv_sem=tab_recv.at[GROUP_OF[(-d) % NZ]],
            device_id=z_peer(d), device_id_type=MESH,
        )
        tab.start()
        tabs.append(tab)
    tabz[0] = tab_ref[z]
    for j in range(NZ):
        zbufs[j][SPANS] = jnp.zeros((2 * SPAN, FEATS), jnp.bfloat16)

    for i in (0, 1):
        locals_[i].wait()
        swaps[i].wait_recv()

    def pack(i, carry):
        rows = pl.ds(pl.multiple_of(2 * SPAN * i, 2 * SPAN), 2 * SPAN)
        qpair = qrows[rows, :].astype(jnp.float32)
        gpair = grows[rows, :].astype(jnp.float32)
        zbufs[0][2 * i] = jnp.concatenate([qpair[:SPAN], gpair[:SPAN]], axis=0).astype(jnp.bfloat16)
        zbufs[0][2 * i + 1] = jnp.concatenate([qpair[SPAN:], gpair[SPAN:]], axis=0).astype(
            jnp.bfloat16
        )
        return carry

    lax.fori_loop(0, SPANS // 2, pack, 0)

    def ring(direction, step):
        src_j = 0 if step == 1 else 2 * (step - 1) - 1 + direction
        dst_j = 7 if step == 4 else 2 * step - 1 + direction
        lo, n = (direction * (SPANS // 2), SPANS // 2) if step == 4 else (0, SPANS)
        return pltpu.make_async_remote_copy(
            src_ref=zbufs[src_j].at[pl.ds(lo, n)], dst_ref=zbufs[dst_j].at[pl.ds(lo, n)],
            send_sem=ring_send.at[direction, step - 1], recv_sem=ring_recv.at[direction, step - 1],
            device_id=z_peer(1 if direction == 0 else -1), device_id_type=MESH,
        )

    rings = {(1, d): ring(d, 1) for d in range(2)}
    for d in range(2):
        rings[1, d].start()

    for tab in tabs:
        tab.wait_recv()
    fetch = pltpu.make_async_copy(tabz, tab_smem, local_sem.at[4])
    fetch.start()
    fetch.wait()

    def spread(j):
        def one(o, carry):
            t = plane_of(o)
            sbuf[j, o - 1] = zbufs[j][tab_smem[j, 0, t]]
            pltpu.make_async_remote_copy(
                src_ref=sbuf.at[j, o - 1], dst_ref=rbuf.at[j, t0],
                send_sem=plane_send.at[j], recv_sem=plane_recv.at[j],
                device_id=(z * PLANE + t, head), device_id_type=MESH,
            ).start()
            return carry

        lax.fori_loop(1, PLANE, one, 0)
        rbuf[j, t0] = zbufs[j][tab_smem[j, 0, t0]]

    spread(0)
    for step in range(1, 5):
        for d in range(2):
            rings[step, d].wait_recv()
            if step < 4:
                rings[step + 1, d] = ring(d, step + 1)
                rings[step + 1, d].start()
        if step < 4:
            spread(2 * step - 1)
            spread(2 * step)
        else:
            spread(7)

    for j in range(NZ):
        arrived = rbuf.at[j, pl.ds(0, PLANE - 1)]
        pltpu.make_async_copy(arrived, arrived, plane_recv.at[j]).wait()
        sent = sbuf.at[j]
        pltpu.make_async_copy(sent, sent, plane_send.at[j]).wait()
    for pending in rings.values():
        pending.wait_send()
    for tab in tabs:
        tab.wait_send()
    for i in (2, 3):
        locals_[i].wait()
        swaps[i].wait_recv()
    for swap in swaps:
        swap.wait_send()


def dispatch(queries, grad_out, new_keys, new_values, table):
    rows = jax.ShapeDtypeStruct((ROWS, FEATS), jnp.bfloat16)
    vmem = pl.BlockSpec(memory_space=pltpu.VMEM)
    hbm = pl.BlockSpec(memory_space=pl.ANY)
    dma = pltpu.SemaphoreType.DMA
    return pl.pallas_call(
        dispatch_kernel,
        out_shape=(
            jax.ShapeDtypeStruct((NZ, PLANE, 2 * SPAN, FEATS), jnp.bfloat16), rows, rows, rows, rows,
        ),
        in_specs=[hbm, hbm, hbm, hbm, vmem],
        out_specs=(vmem,) * 5,
        scratch_shapes=[
            [pltpu.VMEM((SPANS + 1, 2 * SPAN, FEATS), jnp.bfloat16)] * NZ,
            pltpu.VMEM((NZ, PLANE - 1, 2 * SPAN, FEATS), jnp.bfloat16),
            pltpu.VMEM((NZ, SPAN, 128), jnp.int32),
            pltpu.SMEM((NZ, SPAN, 128), jnp.int32),
            dma((4,)), dma((4,)), dma((5,)), dma((NZ,)), dma((NZ,)), dma((2, 4)), dma((2, 4)),
            dma((NZ,)), dma((NZ,)),
        ],
        compiler_params=pltpu.CompilerParams(
            collective_id=0, has_side_effects=True, vmem_limit_bytes=40 * 1024 * 1024
        ),
    )(queries, grad_out, new_keys, new_values, table)


def block_stats(query_tile, grad_tile, key_rows, value_rows, scaling, causal_mask):
    scores = (
        jnp.einsum("rhd,khd->hrk", query_tile, key_rows, preferred_element_type=jnp.float32)
        * scaling
    )
    if causal_mask is not None:
        scores = jnp.where(causal_mask[None], scores, -jnp.inf)
    highest = jnp.max(scores, axis=2)
    weights = jnp.exp(scores - highest[:, :, None])
    totals = jnp.sum(weights, axis=2)
    grad_weights = jnp.einsum(
        "rhd,khd->hrk", grad_tile, value_rows, preferred_element_type=jnp.float32
    )
    inners = jnp.sum(weights * grad_weights, axis=2)
    return (highest + jnp.log(totals)).T, (inners / totals).T


def block_grads(
    query_tile, grad_tile, key_rows, value_rows, log_norm, deltas, scaling, causal_mask
):
    scores = (
        jnp.einsum("rhd,khd->hrk", query_tile, key_rows, preferred_element_type=jnp.float32)
        * scaling
    )
    if causal_mask is not None:
        scores = jnp.where(causal_mask[None], scores, -jnp.inf)
    weights = jnp.exp(scores - log_norm.T[:, :, None])
    grad_weights = jnp.einsum(
        "rhd,khd->hrk", grad_tile, value_rows, preferred_element_type=jnp.float32
    )
    grad_scores = weights * (grad_weights - deltas.T[:, :, None])
    weights_low = weights.astype(jnp.bfloat16)
    grad_low = grad_scores.astype(jnp.bfloat16)
    grad_query = (
        jnp.einsum("hrk,khd->rhd", grad_low, key_rows, preferred_element_type=jnp.float32) * scaling
    )
    grad_keys = (
        jnp.einsum("hrk,rhd->khd", grad_low, query_tile, preferred_element_type=jnp.float32)
        * scaling
    )
    grad_values = jnp.einsum(
        "hrk,rhd->khd", weights_low, grad_tile, preferred_element_type=jnp.float32
    )
    return (grad_query, grad_keys, grad_values)


def body(queries, new_keys, new_values, grad_out, cache_keys, cache_values, choices):
    devices = lax.axis_size("seq")
    z = lax.axis_index("seq") // PLANE
    scaling = 1.0 / math.sqrt(DH)
    flat_picks = choices.reshape(-1)
    hits = choices[:, :, None] == jnp.arange(devices, dtype=jnp.int32)[None, None, :]
    span_ids = jnp.arange(SPANS, dtype=jnp.int32)[:, None, None]
    span_for = jnp.min(jnp.where(hits, span_ids, SPANS), axis=(0, 1))
    table = jnp.pad(span_for.reshape(NZ, 1, PLANE), ((0, 0), (0, 0), (0, 128 - PLANE)))
    table = jnp.broadcast_to(table, (NZ, SPAN, 128))
    received, query_rows, grad_rows, own_keys, own_values = dispatch(
        queries, grad_out, new_keys, new_values, table
    )
    work_query = received[:, :, :SPAN].reshape(devices * SPAN, HEADS, DH)
    work_grad = received[:, :, SPAN:].reshape(devices * SPAN, HEADS, DH)
    key_rows = cache_keys.reshape(-1, HEADS, DH)
    value_rows = cache_values.reshape(-1, HEADS, DH)
    to_sources = jnp.asarray(GROUP_OF, jnp.int32)[(jnp.arange(NZ, dtype=jnp.int32) - z) % NZ]
    to_groups = (z + jnp.asarray(OFFSETS, jnp.int32)) % NZ

    def regroup(slots, order):
        return jnp.take(slots.reshape(NZ, -1), order, axis=0).reshape(slots.shape)

    def exchange(slots):
        return lax.all_to_all(slots, "seq", split_axis=0, concat_axis=0, tiled=True)

    def per_pick(returned):
        return jnp.take(returned, flat_picks, axis=0).reshape(SPANS, TOPK, SPAN, -1)

    block_log, block_delta = block_stats(
        work_query, work_grad, key_rows, value_rows, scaling, None
    )
    stats = jnp.concatenate([block_log, block_delta], axis=1).reshape(devices, SPAN, 2 * HEADS)
    pick_stats = per_pick(exchange(regroup(stats, to_sources)))
    places = jnp.arange(ROWS, dtype=jnp.int32)
    causal = places[None, :] <= places[:, None]
    own_query = query_rows.reshape(ROWS, HEADS, DH)
    own_grad = grad_rows.reshape(ROWS, HEADS, DH)
    own_key_rows = own_keys.reshape(ROWS, HEADS, DH)
    own_value_rows = own_values.reshape(ROWS, HEADS, DH)
    own_log, own_delta = block_stats(
        own_query, own_grad, own_key_rows, own_value_rows, scaling, causal
    )
    logs = jnp.concatenate(
        [own_log.reshape(SPANS, 1, SPAN, HEADS), pick_stats[..., :HEADS]], axis=1
    )
    shares = jnp.concatenate(
        [own_delta.reshape(SPANS, 1, SPAN, HEADS), pick_stats[..., HEADS:]], axis=1
    )
    peak = jnp.max(logs, axis=1)
    log_norm = peak + jnp.log(jnp.sum(jnp.exp(logs - peak[:, None]), axis=1))
    deltas = jnp.sum(shares * jnp.exp(logs - log_norm[:, None]), axis=1)
    joint = jnp.concatenate([log_norm, deltas], axis=2)
    joint_slots = jnp.take(
        jnp.pad(joint, ((0, 1), (0, 0), (0, 0))), span_for, axis=0
    )
    work_joint = regroup(exchange(joint_slots), to_groups).reshape(devices * SPAN, 2 * HEADS)
    grad_slots, sum_keys, sum_values = block_grads(
        work_query, work_grad, key_rows, value_rows, work_joint[:, :HEADS], work_joint[:, HEADS:],
        scaling, None,
    )
    grad_slots = grad_slots.astype(jnp.bfloat16).reshape(devices, SPAN, FEATS)
    pick_grads = per_pick(exchange(regroup(grad_slots, to_sources)))
    own_gq, own_gk, own_gv = block_grads(
        own_query, own_grad, own_key_rows, own_value_rows,
        log_norm.reshape(ROWS, HEADS), deltas.reshape(ROWS, HEADS), scaling, causal,
    )
    pick_sum = jnp.sum(pick_grads.astype(jnp.float32), axis=1).reshape(ROWS, FEATS)
    grad_queries = (own_gq.reshape(ROWS, FEATS) + pick_sum).astype(jnp.bfloat16)
    return (
        grad_queries,
        own_gk.reshape(ROWS, FEATS).astype(jnp.bfloat16),
        own_gv.reshape(ROWS, FEATS).astype(jnp.bfloat16),
        sum_keys.reshape(-1, FEATS).astype(jnp.bfloat16),
        sum_values.reshape(-1, FEATS).astype(jnp.bfloat16),
    )


def solution(mesh):
    rows = P(("seq", "head"), None)
    both = P("seq", "head")
    return jax.shard_map(
        body,
        mesh=mesh,
        in_specs=(rows, rows, rows, rows, both, both, P("seq", None)),
        out_specs=(both,) * 5,
        check_vma=False,
    )
```

time: 412 us -> 258 us (0.63); the launches traced: 406 us -> 258 us
  waiting for transfers between devices: 140 us -> 40.5 us
  blocking collectives: 72.7 us -> 0 us
  Pallas kernels: 0 us -> 69.8 us
  starting transfers between devices: 62.7 us -> 23.5 us
  local copies, waits for them, and re-layouts: 76 us -> 52.8 us
  matrix products: 29.6 us -> 44.2 us
    all_to_all x10 -> x3, waiting for transfers between devices: 140 us -> 40.5 us  [exchange(): return lax.all_to_all(slots, 'seq', split_axis=0, concat_axis=0, tiled=True)]
    all_to_all x2 -> x0, blocking collectives: 72.7 us -> none  [the longest x1 68.8 us: body(): lax.all_to_all(send_grad, 'seq', split_axis=0, concat_axis=0, tiled=True)]
    pallas_call x0 -> x1, Pallas kernels: none -> 69.8 us  [dispatch(): pl.pallas_call(dispatch_kernel, out_shape=(jax.ShapeDtypeStruct((NZ, PLAN...]
    all_to_all x10 -> x3, starting transfers between devices: 62.7 us -> 23.5 us  [exchange(): return lax.all_to_all(slots, 'seq', split_axis=0, concat_axis=0, tiled=True)]
    while x44 -> x0, local copies, waits for them, and re-layouts: 13.6 us -> none
    convert_element_type x1 -> x2, other arithmetic: 1.3 us -> 12.1 us  [block_grads(): grad_low = grad_scores.astype(jnp.bfloat16)]
    dot_general x2 -> x1, matrix products: 3.83 us -> 11.3 us  [block_stats(): jnp.einsum('rhd,khd->hrk', grad_tile, value_rows, preferred_element_type=...]
    dot_general x2 -> x1, matrix products: 2.53 us -> 9.79 us  [block_stats(): jnp.einsum('rhd,khd->hrk', query_tile, key_rows, preferred_element_type=j...]
  transfers between devices with their start and end apart: 10 -> 3, of which waited for: 8 -> 3; matrix products, arithmetic and copies ran while one was open for 13% -> 13% of each run, Pallas kernels for 0% -> 0%
where the time goes in v1:
time: 258 us
  Pallas kernels  69.8 us (27%)
  local copies, waits for them, and re-layouts  52.8 us (20%)
  matrix products  44.2 us (17%)
  waiting for transfers between devices  40.5 us (16%)
  other arithmetic  25.6 us (10%)
  starting transfers between devices  23.5 us (9%)
    pallas_call x1, Pallas kernels, dispatch(): pl.pallas_call(dispatch_kernel, out_shape=(jax.ShapeDtypeStruct((NZ, PLAN...  69.8 us
    all_to_all x3, waiting for transfers between devices, exchange(): return lax.all_to_all(slots, 'seq', split_axis=0, concat_axis=0, tiled=True)  40.5 us
    all_to_all x3, starting transfers between devices, exchange(): return lax.all_to_all(slots, 'seq', split_axis=0, concat_axis=0, tiled=True)  23.5 us
    unnamed x60, local copies, waits for them, and re-layouts  19.2 us
    convert_element_type x2, other arithmetic, block_grads(): grad_low = grad_scores.astype(jnp.bfloat16)  12.1 us
    dot_general x1, matrix products, block_stats(): jnp.einsum('rhd,khd->hrk', grad_tile, value_rows, preferred_element_type=...  11.3 us
    dot_general x2, matrix products, block_grads(): jnp.einsum('hrk,rhd->khd', weights_low, grad_tile, preferred_element_type...  11.1 us
    dot_general x1, matrix products, block_stats(): jnp.einsum('rhd,khd->hrk', query_tile, key_rows, preferred_element_type=j...  9.79 us
  transfers between devices with their start and end apart: 3, of which 3 were waited for; matrix products, arithmetic and copies ran while one was open for 13% of the time, Pallas kernels for 0%

profile of v1, /device:TPU:32, one launch (start us, length us, event | category | flops | bytes accessed | tf_op | source)
XLA Modules:
  0.0 257.7 jit_solution(14028662706518481364)
XLA Ops:
  0.7 1.4 gather_fusion
  2.1 0.8 select_reduce_fusion
  3.0 0.9 copy-done.1
  3.9 0.9 copy-done.2
  4.9 0.9 copy-done.3
  5.8 0.9 copy-done.4
  6.8 69.8 %shard_map.128 = (bf16[8,16,16,1024]{3,2,1,0:T(8,128)(2,1)S(1)}, bf16[128,1024]{1,0:T(8,128)(2,1)S(1)}, bf16[128,1024]{1,0:T(8,128)(2,1)S(1)}, bf16[128,1024]{1,0:T(8,128)(2,1)S(1)}, bf16[128,1024]{1,0:T(8,128)(2,1)S(1)}) custom-call(bf16[64,2048]{1,0:T(8,128)(2,1)S(1)} %copy-done.1, bf16[64,2048]{1,0:T(8,128)(2,1)S(1)} %copy-done.2, ...), custom_call_target="tpu_custom_call" | custom-call | tf_op jit(solution)/shard_map/pallas_call | solution.py:177
  76.6 1.8 fusion.38
  78.4 1.9 copy.244
  80.4 4.1 %copy.215 = bf16[1024,8,128]{0,2,1:T(8,128)(2,1)} copy(bf16[1024,8,128]{2,1,0:T(8,128)(2,1)} %bitcast.119) | data formatting | bytes 4194304 | tf_op jit(solution)/shard_map/reshape | solution.py:257
  84.5 3.5 %copy.245 = bf16[128,8,8,128]{3,2,1,0:T(8,128)(2,1)} copy(bf16[128,8,8,128]{3,1,2,0:T(8,128)(2,1)} %bitcast.121) | data formatting | bytes 4194304
  88.0 4.2 %copy.217 = bf16[1024,8,128]{0,2,1:T(8,128)(2,1)} copy(bf16[1024,8,128]{2,1,0:T(8,128)(2,1)} %bitcast.120) | data formatting | bytes 4194304 | tf_op jit(solution)/shard_map/reshape | solution.py:258
  92.2 9.8 %multiply_reduce_fusion.1 = (f32[8,1024]{1,0:T(8,128)S(1)}, f32[8,1024,512]{1,2,0:T(8,128)}) fusion(bf16[1024,8,128]{0,2,1:T(8,128)(2,1)} %copy.215, bf16[512,1024]{1,0:T(8,128)(2,1)S(1)} %copy-done), kind=kOutput, calls=%fused_computation.14 | convolution fusion | flops 1082122240 | bytes 19955712 | tf_op jit(solution)/shard_map/rhd,khd->hrk/dot_general | solution.py:200
  102.0 11.3 %fusion = (f32[8,1024]{1,0:T(8,128)S(1)}, f32[8,1024]{1,0:T(8,128)S(1)}, f32[8,1024,512]{1,2,0:T(8,128)}) fusion(f32[8,1024,512]{1,2,0:T(8,128)} %get-tuple-element.63, f32[8,1024]{1,0:T(8,128)S(1)} %get-tuple-element.62, bf16[1024,8,128]{0,2,1:T(8,128)(2,1)S(1)} %copy-done.7, bf16[512,1024]{1,0:T(8,128)(2,1)S(1)} %copy-done.18), kind=kOutput, calls=%fused_computation.12 | convolution fusion | flops 1094696960 | bytes 36798464 | tf_op jit(solution)/shard_map/rhd,khd->hrk/dot_general | solution.py:208
  114.7 0.9 reshape.333
  115.6 9.0 %all-to-all-start = ((f32[128,1,128]{2,1,0:T(1,128)}), f32[128,1,128]{2,1,0:T(1,128)S(1)}, u32[]{:S(2)}, u32[]{:S(2)}) async-start(f32[128,1,128]{2,1,0:T(1,128)} %reshape.333), calls=%async_computation | async-start | bytes 131072 | tf_op jit(solution)/shard_map/all_to_all | solution.py:268
  127.5 1.0 fusion.23
  128.8 7.2 %all-to-all-done = f32[128,1,128]{2,1,0:T(1,128)S(1)} async-done(((f32[128,1,128]{2,1,0:T(1,128)}), f32[128,1,128]{2,1,0:T(1,128)S(1)}, u32[]{:S(2)}, u32[]{:S(2)}) %all-to-all-start) | async-done | bytes 65568 | tf_op jit(solution)/shard_map/all_to_all | solution.py:268
  136.5 0.8 reduce.2
  139.3 0.8 gather_fusion.2
  140.1 0.9 broadcast_select_fusion.1
  140.9 0.9 reshape.335
  141.8 6.6 %all-to-all-start.1 = ((f32[128,1,128]{2,1,0:T(1,128)}), f32[128,1,128]{2,1,0:T(1,128)S(1)}, u32[]{:S(2)}, u32[]{:S(2)}) async-start(f32[128,1,128]{2,1,0:T(1,128)} %reshape.335), calls=%async_computation.1 | async-start | bytes 131072 | tf_op jit(solution)/shard_map/all_to_all | solution.py:268
  149.1 0.7 broadcast_in_dim.113
  150.5 9.2 %all-to-all-done.1 = f32[128,1,128]{2,1,0:T(1,128)S(1)} async-done(((f32[128,1,128]{2,1,0:T(1,128)}), f32[128,1,128]{2,1,0:T(1,128)S(1)}, u32[]{:S(2)}, u32[]{:S(2)}) %all-to-all-start.1) | async-done | bytes 65568 | tf_op jit(solution)/shard_map/all_to_all | solution.py:268
  159.8 0.8 reduce.3
  161.6 0.7 broadcast_select_fusion.3
  163.0 12.0 %multiply_convert_fusion = bf16[8,1024,512]{1,2,0:T(8,128)(2,1)S(1)} fusion(f32[8,1024,512]{1,2,0:T(8,128)} %get-tuple-element.64, f32[8,1024,512]{1,2,0:T(8,128)} %get-tuple-element.63, f32[8,1024]{1,0:T(8,128)S(1)} %copy.204, f32[8,1024]{1,0:T(8,128)S(1)} %copy.203), kind=kLoop, calls=%fused_computation.8 | loop fusion | flops 20971520 | bytes 42008576 | tf_op jit(solution)/shard_map/convert_element_type | solution.py:230
  175.0 2.7 %fusion.6 = bf16[1024,8,128]{2,0,1:T(8,128)(2,1)S(1)} fusion(bf16[8,1024,512]{1,2,0:T(8,128)(2,1)S(1)} %multiply_convert_fusion, bf16[512,1024]{1,0:T(8,128)(2,1)S(1)} %copy-done), kind=kOutput, calls=%fused_computation.22 | convolution fusion | flops 1075838976 | bytes 11534336 | tf_op jit(solution)/shard_map/hrk,khd->rhd/dot_general | solution.py:232
  178.2 1.4 copy.207
  179.6 2.2 reshape_reshape.11
  181.8 1.7 fusion.39
  183.5 2.2 gather_fusion.4
  185.7 2.2 gather_fusion.5
  187.9 1.7 pad_maximum_fusion
  189.6 2.3 gather.36
  191.9 3.3 %broadcast_select_fusion = bf16[128,8,1024]{2,1,0:T(8,128)(2,1)} fusion(bf16[128,8,1024]{2,1,0:T(8,128)(2,1)} %gather.36, pred[128]{0:T(512)(128)(4,1)S(1)} %broadcast_in_dim.114), kind=kLoop, calls=%fused_computation.21 | loop fusion | flops 1048576 | bytes 4194432 | tf_op jit(solution)/shard_map/jit(_take)/select_n | solution.py:265
  195.2 7.9 %all-to-all-start.2 = ((bf16[128,8,1024]{2,1,0:T(8,128)(2,1)}), bf16[128,8,1024]{2,1,0:T(8,128)(2,1)}, u32[]{:S(2)}, u32[]{:S(2)}) async-start(bf16[128,8,1024]{2,1,0:T(8,128)(2,1)} %broadcast_select_fusion), calls=%async_computation.2 | async-start | bytes 4194304 | tf_op jit(solution)/shard_map/all_to_all | solution.py:268
  203.5 0.9 copy.221
  205.0 0.9 copy.220
  206.2 1.0 copy.201
  207.2 10.8 %fusion.7 = bf16[8,128,512]{2,1,0:T(8,128)(2,1)} fusion(bf16[1024,8,128]{0,2,1:T(8,128)(2,1)} %copy.217, f32[8,1024,512]{1,2,0:T(8,128)} %get-tuple-element.63, f32[8,1024]{1,0:T(8,128)} %copy-done.19), kind=kOutput, calls=%fused_computation.24 | convolution fusion | flops 1086849024 | bytes 19955712 | tf_op jit(solution)/shard_map/hrk,rhd->khd/dot_general | solution.py:238
  218.0 2.3 copy.223
  220.3 7.3 %multiply_convert_fusion.2 = bf16[8,128,512]{2,1,0:T(8,128)(2,1)} fusion(bf16[1024,8,128]{0,2,1:T(8,128)(2,1)S(1)} %copy-done.6, bf16[8,1024,512]{1,2,0:T(8,128)(2,1)} %copy-done.5), kind=kOutput, calls=%fused_computation.20 | convolution fusion | flops 1074790400 | bytes 11534336 | tf_op jit(solution)/shard_map/hrk,rhd->khd/dot_general | solution.py:235
  227.6 2.3 copy.222
  229.9 24.1 %all-to-all-done.2 = bf16[128,8,1024]{2,1,0:T(8,128)(2,1)} async-done(((bf16[128,8,1024]{2,1,0:T(8,128)(2,1)}), bf16[128,8,1024]{2,1,0:T(8,128)(2,1)}, u32[]{:S(2)}, u32[]{:S(2)}) %all-to-all-start.2) | async-done | bytes 2097184 | tf_op jit(solution)/shard_map/all_to_all | solution.py:268
  254.0 2.2 gather_fusion.3
  256.8 0.8 copy.219
  (110 shorter events, 12.6 us)
Async XLA Ops:
  0.6 91.6 %copy-start = (bf16[512,1024]{1,0:T(8,128)(2,1)S(1)}, bf16[512,1024]{1,0:T(8,128)(2,1)}, u32[]{:S(2)}) copy-start(bf16[512,1024]{1,0:T(8,128)(2,1)} %param.15) | copy-start | bytes 3145732
  2.1 112.4 %copy-start.22 = (pred[8]{0:T(512)(128)(4,1)}, pred[8]{0:T(512)(128)(4,1)S(1)}, u32[]{:S(2)}) copy-start(pred[8]{0:T(512)(128)(4,1)S(1)} %compare_and_fusion.1) | copy-start | bytes 28
  3.0 1.0 copy-start.1
  3.9 0.9 copy-start.2
  4.9 0.9 copy-start.3
  5.8 0.9 copy-start.4
  92.2 9.8 %copy-start.7 = (bf16[1024,8,128]{0,2,1:T(8,128)(2,1)S(1)}, bf16[1024,8,128]{0,2,1:T(8,128)(2,1)}, u32[]{:S(2)}) copy-start(bf16[1024,8,128]{0,2,1:T(8,128)(2,1)} %copy.217) | copy-start | bytes 6291460
  92.2 9.8 %copy-start.18 = (bf16[512,1024]{1,0:T(8,128)(2,1)S(1)}, bf16[512,1024]{1,0:T(8,128)(2,1)}, u32[]{:S(2)}) copy-start(bf16[512,1024]{1,0:T(8,128)(2,1)} %param.16) | copy-start | bytes 3145732
  102.0 22.6 %copy-start.21 = (s32[16,3]{0,1:T(4,128)S(1)}, s32[16,3]{0,1:T(4,128)}, u32[]{:S(2)}) copy-start(s32[16,3]{0,1:T(4,128)} %param.17) | copy-start | bytes 580
  113.3 13.2 %copy-start.23 = (s32[8]{0:T(128)S(1)}, s32[8]{0:T(128)}, u32[]{:S(2)}) copy-start(s32[8]{0:T(128)} %constant.126.clone) | copy-start | bytes 100
  115.6 20.4 %all-to-all-start = ((f32[128,1,128]{2,1,0:T(1,128)}), f32[128,1,128]{2,1,0:T(1,128)S(1)}, u32[]{:S(2)}, u32[]{:S(2)}) async-start(f32[128,1,128]{2,1,0:T(1,128)} %reshape.333), calls=%async_computation | async-start | bytes 131072 | tf_op jit(solution)/shard_map/all_to_all | solution.py:268
  126.1 13.9 %copy-start.12 = (bf16[128,1024]{0,1:T(8,128)(2,1)}, bf16[128,1024]{0,1:T(8,128)(2,1)S(1)}, u32[]{:S(2)}) copy-start(bf16[128,1024]{0,1:T(8,128)(2,1)S(1)} %copy.238) | copy-start | bytes 786436
  126.3 13.7 %copy-start.10 = (bf16[128,1024]{0,1:T(8,128)(2,1)}, bf16[128,1024]{0,1:T(8,128)(2,1)S(1)}, u32[]{:S(2)}) copy-start(bf16[128,1024]{0,1:T(8,128)(2,1)S(1)} %copy.239) | copy-start | bytes 786436
  126.5 14.4 %copy-start.14 = (bf16[128,1024]{0,1:T(8,128)(2,1)}, bf16[128,1024]{0,1:T(8,128)(2,1)S(1)}, u32[]{:S(2)}) copy-start(bf16[128,1024]{0,1:T(8,128)(2,1)S(1)} %copy.240) | copy-start | bytes 786436
  127.5 1.0 copy-start.8
  141.8 18.0 %all-to-all-start.1 = ((f32[128,1,128]{2,1,0:T(1,128)}), f32[128,1,128]{2,1,0:T(1,128)S(1)}, u32[]{:S(2)}, u32[]{:S(2)}) async-start(f32[128,1,128]{2,1,0:T(1,128)} %reshape.335), calls=%async_computation.1 | async-start | bytes 131072 | tf_op jit(solution)/shard_map/all_to_all | solution.py:268
  162.9 12.2 %copy-start.19 = (f32[8,1024]{1,0:T(8,128)}, f32[8,1024]{1,0:T(8,128)S(1)}, u32[]{:S(2)}) copy-start(f32[8,1024]{1,0:T(8,128)S(1)} %copy.203) | copy-start | bytes 98308
  175.0 3.2 %copy-start.5 = (bf16[8,1024,512]{1,2,0:T(8,128)(2,1)}, bf16[8,1024,512]{1,2,0:T(8,128)(2,1)S(1)}, u32[]{:S(2)}) copy-start(bf16[8,1024,512]{1,2,0:T(8,128)(2,1)S(1)} %multiply_convert_fusion) | copy-start | bytes 25165828
  191.9 11.2 %copy-start.20 = (f32[128,8]{1,0:T(8,128)S(1)}, f32[128,8]{1,0:T(8,128)}, u32[]{:S(2)}) copy-start(f32[128,8]{1,0:T(8,128)} %get-tuple-element.56) | copy-start | bytes 12292
  191.9 11.3 %copy-start.9 = (f32[8,128,128]{1,2,0:T(8,128)S(1)}, f32[8,128,128]{1,2,0:T(8,128)}, u32[]{:S(2)}) copy-start(f32[8,128,128]{1,2,0:T(8,128)} %copy-done.8) | copy-start | bytes 1572868
  191.9 11.3 %copy-start.15 = (bf16[128,1024]{0,1:T(8,128)(2,1)S(1)}, bf16[128,1024]{0,1:T(8,128)(2,1)}, u32[]{:S(2)}) copy-start(bf16[128,1024]{0,1:T(8,128)(2,1)} %copy-done.14) | copy-start | bytes 786436
  191.9 12.5 %copy-start.16 = (f32[8,128,128]{1,2,0:T(8,128)S(1)}, f32[8,128,128]{1,2,0:T(8,128)}, u32[]{:S(2)}) copy-start(f32[8,128,128]{1,2,0:T(8,128)} %get-tuple-element.67) | copy-start | bytes 1572868
  195.2 9.4 %copy-start.11 = (bf16[128,1024]{0,1:T(8,128)(2,1)S(1)}, bf16[128,1024]{0,1:T(8,128)(2,1)}, u32[]{:S(2)}) copy-start(bf16[128,1024]{0,1:T(8,128)(2,1)} %copy-done.10) | copy-start | bytes 786436
  195.2 10.7 %copy-start.13 = (bf16[128,1024]{0,1:T(8,128)(2,1)S(1)}, bf16[128,1024]{0,1:T(8,128)(2,1)}, u32[]{:S(2)}) copy-start(bf16[128,1024]{0,1:T(8,128)(2,1)} %copy-done.12) | copy-start | bytes 786436
  195.2 58.9 %all-to-all-start.2 = ((bf16[128,8,1024]{2,1,0:T(8,128)(2,1)}), bf16[128,8,1024]{2,1,0:T(8,128)(2,1)}, u32[]{:S(2)}, u32[]{:S(2)}) async-start(bf16[128,8,1024]{2,1,0:T(8,128)(2,1)} %broadcast_select_fusion), calls=%async_computation.2 | async-start | bytes 4194304 | tf_op jit(solution)/shard_map/all_to_all | solution.py:268
  207.2 13.1 %copy-start.6 = (bf16[1024,8,128]{0,2,1:T(8,128)(2,1)S(1)}, bf16[1024,8,128]{0,2,1:T(8,128)(2,1)}, u32[]{:S(2)}) copy-start(bf16[1024,8,128]{0,2,1:T(8,128)(2,1)} %copy.215) | copy-start | bytes 6291460
  227.6 29.2 %copy-start.17 = (f32[128,8,128]{0,2,1:T(8,128)S(1)}, f32[128,8,128]{0,2,1:T(8,128)}, u32[]{:S(2)}) copy-start(f32[128,8,128]{0,2,1:T(8,128)} %copy.201) | copy-start | bytes 1572868

commit v2 on v1

v2 whole, which is shorter than its diff:
```python
import math

import jax
import jax.numpy as jnp
from jax import lax
from jax.experimental import pallas as pl
from jax.experimental.pallas import tpu as pltpu
from jax.sharding import PartitionSpec as P

DH = 128
SPAN = 8
TOPK = 3
NZ = 8
NX = 4
NY = 4
PLANE = NX * NY
SPANS = 16
FEATS = 1024
HEADS = FEATS // DH
ROWS = SPANS * SPAN
BLK = 512
PAIRS = NZ // 2
PAIR_ROWS = 2 * PLANE * SPAN
UNIT = 2 * SPAN
CHUNKS = 4
CHUNK = SPANS // CHUNKS
SCALING = 1.0 / math.sqrt(DH)
LOG2E = math.log2(math.e)
SCALING2 = SCALING * LOG2E
MESH = pl.DeviceIdType.MESH
OFFSETS = (-1, 1, -2, 2, -3, 3, 0, 4)
GROUP_OF = (6, 1, 3, 5, 7, 4, 2, 0)
OWN = 6
FAR = 7
TAB_A, TAB_B, TAB_S, TAB_END = 0, 256, 384, 512
BF16 = jnp.bfloat16
F32 = jnp.float32
HIGHEST = lax.Precision.HIGHEST


def iota(shape, axis):
    return lax.broadcasted_iota(jnp.int32, shape, axis)


def nt(a, b, precision=None):
    return lax.dot_general(
        a, b, (((1,), (1,)), ((), ())), precision=precision, preferred_element_type=F32
    )


def tn(a, b, precision=None):
    return lax.dot_general(
        a, b, (((0,), (0,)), ((), ())), precision=precision, preferred_element_type=F32
    )


def nn(a, b, precision=None):
    return jnp.dot(a, b, precision=precision, preferred_element_type=F32)


def lane_mask(lanes):
    return iota((128, lanes), 0) // 16 == iota((128, lanes), 1) % SPAN


def pick_pair(p):
    row, lane = iota((128, PAIR_ROWS), 0), iota((128, PAIR_ROWS), 1)
    hit = (row // NZ == lane // UNIT) & (row % NZ == 2 * p + (lane // SPAN) % 2)
    return hit.astype(F32)


def pick_own():
    return (iota((SPANS, ROWS), 0) == iota((SPANS, ROWS), 1) // SPAN).astype(F32)


def stacked(stats):
    tall = jnp.concatenate([stats] * SPAN, axis=0)
    return jnp.where(lane_mask(stats.shape[1]), tall, 0.0)


def unstacked(wide):
    kept = jnp.where(lane_mask(wide.shape[1]), wide, 0.0)
    return jnp.sum(kept.reshape(SPAN, 2 * HEADS, wide.shape[1]), axis=0)


def head_cols(h):
    return pl.ds(pl.multiple_of(h * DH, DH), DH)


def kernel(
    q_hbm, g_hbm, k_hbm, v_hbm, ck_hbm, cv_hbm, tab_ref, sel_ref,
    gq_out, gnk_out, gnv_out, gck_hbm, gcv_hbm,
    own_q, own_g, own_k, own_v, kc, vc, kt,
    zbufs, sbuf, rbuf, tabz, tab_smem, qs, gs, wl, gl,
    stat, own_stat, st_out, st_in, zst_out, zst_in, nz, nr_out, nr_in, joint, own_joint,
    gqb, gr, rs_out, rs_in, own_gq, gck, gcv,
    head_send, head_recv, local_sem, tab_send, tab_recv, ring_send, ring_recv,
    plane_send, plane_recv, st_send, st_recv, zst_send, zst_recv, nz_send, nz_recv,
    nr_send, nr_recv, gr_send, gr_recv, rs_send, rs_recv,
):
    seq = lax.axis_index("seq")
    head = lax.axis_index("head")
    z = seq // PLANE
    t0 = seq % PLANE
    x0 = t0 // NY
    y0 = t0 % NY

    def z_peer(d):
        return (((z + d) % NZ) * PLANE + t0, head)

    def plane_of(o):
        return ((x0 + o // NY) % NX) * NY + (y0 + o % NY) % NY

    def plane_peer(t):
        return (z * PLANE + t, head)

    def remote(src, dst, send, recv, device):
        return pltpu.make_async_remote_copy(
            src_ref=src, dst_ref=dst, send_sem=send, recv_sem=recv,
            device_id=device, device_id_type=MESH,
        )

    def await_bytes(ref, sem):
        pltpu.make_async_copy(ref, ref, sem).wait()

    fetch_k = pltpu.make_async_copy(ck_hbm, kc, local_sem.at[5])
    fetch_v = pltpu.make_async_copy(cv_hbm, vc, local_sem.at[6])
    half = ROWS // 2
    my_rows = pl.ds(pl.multiple_of(head * half, half), half)
    my_cols = pl.ds(pl.multiple_of(head * FEATS, FEATS), FEATS)
    other_cols = pl.ds(pl.multiple_of((1 - head) * FEATS, FEATS), FEATS)
    sources = ((q_hbm, own_q), (g_hbm, own_g), (k_hbm, own_k), (v_hbm, own_v))
    keeps = [
        pltpu.make_async_copy(src.at[:, my_cols], dst.at[my_rows, :], local_sem.at[i])
        for i, (src, dst) in enumerate(sources)
    ]
    for keep in keeps:
        keep.start()

    sibling = (seq, 1 - head)
    barrier = pltpu.get_barrier_semaphore()
    pl.semaphore_signal(barrier, inc=1, device_id=sibling, device_id_type=MESH)
    for d in range(1, NZ):
        pl.semaphore_signal(barrier, inc=1, device_id=z_peer(d), device_id_type=MESH)

    def greet(o, carry):
        pl.semaphore_signal(
            barrier, inc=1, device_id=plane_peer(plane_of(o)), device_id_type=MESH
        )
        return carry

    lax.fori_loop(1, PLANE, greet, 0)
    for i in range(NZ):
        zbufs[i][SPANS] = jnp.zeros((UNIT, FEATS), BF16)
    tabz[OWN] = tab_ref[z]
    pl.semaphore_wait(barrier, 1 + (NZ - 1) + (PLANE - 1))

    swaps = [
        remote(src.at[:, other_cols], dst.at[my_rows, :], head_send.at[i], head_recv.at[i], sibling)
        for i, (src, dst) in enumerate(sources)
    ]
    for swap in swaps[:2]:
        swap.start()
    tabs = []
    for d in range(1, NZ):
        i = GROUP_OF[(-d) % NZ]
        tab = remote(tab_ref.at[(z + d) % NZ], tabz.at[i], tab_send.at[d], tab_recv.at[i], z_peer(d))
        tab.start()
        tabs.append(tab)
    for swap in swaps[2:]:
        swap.start()
    fetch_k.start()
    fetch_v.start()
    for i in (0, 1):
        keeps[i].wait()
        swaps[i].wait_recv()

    def pack(i, carry):
        rows = pl.ds(pl.multiple_of(UNIT * i, UNIT), UNIT)
        qpair = own_q[rows, :].astype(F32)
        gpair = own_g[rows, :].astype(F32)
        zbufs[OWN][2 * i] = jnp.concatenate([qpair[:SPAN], gpair[:SPAN]], axis=0).astype(BF16)
        zbufs[OWN][2 * i + 1] = jnp.concatenate([qpair[SPAN:], gpair[SPAN:]], axis=0).astype(BF16)
        return carry

    rings = {}

    def ring(direction, step, chunk):
        src_i = OWN if step == 1 else 2 * (step - 2) + direction
        dst_i = FAR if step == 4 else 2 * (step - 1) + direction
        part = pl.ds(chunk * CHUNK, CHUNK)
        copy = remote(
            zbufs[src_i].at[part], zbufs[dst_i].at[part],
            ring_send.at[direction, step - 1, chunk], ring_recv.at[direction, step - 1, chunk],
            z_peer(1 if direction == 0 else -1),
        )
        copy.start()
        rings[direction, step, chunk] = copy

    for chunk in range(CHUNKS):
        lax.fori_loop(2 * chunk, 2 * chunk + 2, pack, 0)
        for direction in range(2):
            ring(direction, 1, chunk)

    for tab in tabs:
        tab.wait_recv()
    to_smem = pltpu.make_async_copy(
        tabz.at[:, :, pl.ds(TAB_S, TAB_END - TAB_S)], tab_smem, local_sem.at[4]
    )
    to_smem.start()
    to_smem.wait()

    def spread(i):
        def one(o, carry):
            t = plane_of(o)
            sbuf[i, o - 1] = zbufs[i][tab_smem[i, 0, t]]
            remote(
                sbuf.at[i, o - 1], rbuf.at[i, t0], plane_send.at[i], plane_recv.at[i], plane_peer(t)
            ).start()
            return carry

        lax.fori_loop(1, PLANE, one, 0)
        rbuf[i, t0] = zbufs[i][tab_smem[i, 0, t0]]

    def unpack(p):
        for i in (2 * p, 2 * p + 1):
            await_bytes(rbuf.at[i, pl.ds(0, PLANE - 1)], plane_recv.at[i])

        def one(t, carry):
            rows = pl.ds(pl.multiple_of(p * PAIR_ROWS + t * UNIT, UNIT), UNIT)
            a = rbuf[2 * p, t].astype(F32)
            b = rbuf[2 * p + 1, t].astype(F32)
            qs[rows, :] = jnp.concatenate([a[:SPAN], b[:SPAN]], axis=0).astype(BF16)
            gs[rows, :] = jnp.concatenate([a[SPAN:], b[SPAN:]], axis=0).astype(BF16)
            return carry

        lax.fori_loop(0, PLANE, one, 0)

    def pair_rows(p):
        return pl.ds(p * PAIR_ROWS, PAIR_ROWS)

    def first_head(p):
        def one(h, carry):
            cols = head_cols(h)
            scores = nt(kc[:, cols], qs[pair_rows(p), cols]) * SCALING2
            high = jnp.max(scores, axis=0, keepdims=True)
            weights = jnp.exp2(scores - high)
            total = jnp.sum(weights, axis=0, keepdims=True)
            grad_weights = nt(vc[:, cols], gs[pair_rows(p), cols])
            inner = jnp.sum(weights * grad_weights, axis=0, keepdims=True)
            stat[p, pl.ds(h, 1), :] = high + jnp.log(total) * LOG2E
            stat[p, pl.ds(HEADS + h, 1), :] = inner / total
            return carry

        return one

    def own_scores(cols):
        scores = nt(own_k[:, cols], own_q[:, cols]) * SCALING2
        seen = iota((ROWS, ROWS), 0) <= iota((ROWS, ROWS), 1)
        return jnp.where(seen, scores, -jnp.inf)

    def own_first(h, carry):
        cols = head_cols(h)
        scores = own_scores(cols)
        high = jnp.max(scores, axis=0, keepdims=True)
        weights = jnp.exp2(scores - high)
        total = jnp.sum(weights, axis=0, keepdims=True)
        grad_weights = nt(own_v[:, cols], own_g[:, cols])
        inner = jnp.sum(weights * grad_weights, axis=0, keepdims=True)
        own_stat[pl.ds(h, 1), :] = high + jnp.log(total) * LOG2E
        own_stat[pl.ds(HEADS + h, 1), :] = inner / total
        return carry

    def turn_keys(h, carry):
        kt[h] = kc[:, head_cols(h)].T
        return carry

    spread(OWN)
    for i in (2, 3):
        keeps[i].wait()
        swaps[i].wait_recv()
    fetch_k.wait()
    fetch_v.wait()
    for step in range(1, 5):
        if step == 4:
            unpack(1)
        if step == 3:
            unpack(0)
        for chunk in range(CHUNKS):
            for direction in range(2):
                if step == 4 and chunk // 2 != direction:
                    continue
                rings[direction, step, chunk].wait_recv()
                if step < 3 or (step == 3 and chunk // 2 == direction):
                    ring(direction, step + 1, chunk)
            heads = (2 * chunk, 2 * chunk + 2)
            if step == 1:
                lax.fori_loop(*heads, own_first, 0)
            elif step == 2:
                lax.fori_loop(*heads, turn_keys, 0)
            else:
                lax.fori_loop(*heads, first_head(step - 3), 0)
        if step < 4:
            spread(2 * (step - 1))
            spread(2 * (step - 1) + 1)
        else:
            spread(FAR)
    for p in (2, 3):
        unpack(p)
        lax.fori_loop(0, HEADS, first_head(p), 0)

    slot_stats = nt(pick_pair(0), stacked(stat[0]), HIGHEST)
    for p in range(1, PAIRS):
        slot_stats += nt(pick_pair(p), stacked(stat[p]), HIGHEST)
    st_out[...] = slot_stats.reshape(PLANE, NZ, 128)

    def plane_all(out, into, send, recv):
        def one(o, carry):
            t = plane_of(o)
            remote(out.at[t], into.at[t0], send, recv, plane_peer(t)).start()
            return carry

        lax.fori_loop(1, PLANE, one, 0)
        into[t0] = out[t0]

    plane_all(st_out, st_in, st_send.at[0], st_recv.at[0])
    own_slots = nt(pick_own(), stacked(own_stat[...]), HIGHEST)
    row, lane = iota((128, 128), 0), iota((128, 128), 1)
    swap_order = ((row // PLANE == lane % NZ) & (row % PLANE == lane // NZ)).astype(F32)
    await_bytes(st_in.at[pl.ds(0, PLANE - 1)], st_recv.at[0])
    routed = nn(swap_order, st_in[...].reshape(128, 128), HIGHEST)
    zst_out[...] = routed.reshape(NZ, PLANE, 128)
    stats_home = []
    for i in range(NZ):
        j = GROUP_OF[(-OFFSETS[i]) % NZ]
        if i == OWN:
            zst_in[OWN] = zst_out[OWN]
            continue
        copy = remote(
            zst_out.at[i], zst_in.at[j], zst_send.at[i], zst_recv.at[j], z_peer(OFFSETS[i])
        )
        copy.start()
        stats_home.append(copy)
    for copy in stats_home:
        copy.wait_recv()

    chosen = (sel_ref[...] == iota((TOPK * SPANS, 128), 1)).astype(F32)
    picked = nn(chosen, zst_in[...].reshape(128, 128), HIGHEST)
    logs = [own_slots] + [picked[SPANS * t:SPANS * (t + 1)] for t in range(TOPK)]
    peak = jnp.maximum(jnp.maximum(logs[0], logs[1]), jnp.maximum(logs[2], logs[3]))
    shares = [jnp.exp2(log - peak) for log in logs]
    total = (shares[0] + shares[1]) + (shares[2] + shares[3])
    norm = peak + jnp.log(total) * LOG2E
    delta = jnp.zeros((SPANS, 128), F32)
    for share, log in zip(shares, logs):
        delta += pltpu.roll(share / total, HEADS, 1) * log
    is_norm = iota((SPANS, 128), 1) % (2 * HEADS) < HEADS
    nz[OWN] = jnp.where(is_norm, norm, delta)
    norms_out = []
    for d in range(1, NZ):
        i = GROUP_OF[(-d) % NZ]
        copy = remote(nz.at[OWN], nz.at[i], nz_send.at[d], nz_recv.at[i], z_peer(d))
        copy.start()
        norms_out.append(copy)
    own_joint[...] = unstacked(tn(nz[OWN], pick_own(), HIGHEST))
    lane8 = iota((SPANS, 128), 1) % NZ
    span_row = iota((SPANS, 128), 0)
    routes = jnp.concatenate(
        [
            jnp.where((lane8 == i) & (tabz[i, 0:1, TAB_B:TAB_S] == span_row), 1.0, 0.0)
            for i in range(NZ)
        ],
        axis=0,
    ).astype(F32)
    for copy in norms_out:
        copy.wait_recv()
    nr_out[...] = tn(routes, nz[...].reshape(128, 128), HIGHEST).reshape(PLANE, NZ, 128)
    plane_all(nr_out, nr_in, nr_send.at[0], nr_recv.at[0])

    def own_second(h, carry):
        cols = head_cols(h)
        weights = jnp.exp2(own_scores(cols) - own_joint[pl.ds(h, 1), :])
        grad_weights = nt(own_v[:, cols], own_g[:, cols])
        grad_scores = weights * (grad_weights - own_joint[pl.ds(HEADS + h, 1), :])
        weights_low = weights.astype(BF16)
        grad_low = grad_scores.astype(BF16)
        own_gq[:, cols] = tn(grad_low, own_k[:, cols]) * SCALING
        gnk_out[:, cols] = (nn(grad_low, own_q[:, cols]) * SCALING).astype(BF16)
        gnv_out[:, cols] = nn(weights_low, own_g[:, cols]).astype(BF16)
        return carry

    lax.fori_loop(0, HEADS, own_second, 0)
    await_bytes(nr_in.at[pl.ds(0, PLANE - 1)], nr_recv.at[0])

    def second(p):
        joint[p] = unstacked(tn(nr_in[...].reshape(128, 128), pick_pair(p), HIGHEST))

        def one(h, carry):
            cols = head_cols(h)
            scores = nt(kc[:, cols], qs[pair_rows(p), cols]) * SCALING2
            weights = jnp.exp2(scores - joint[p, pl.ds(h, 1), :])
            grad_weights = nt(vc[:, cols], gs[pair_rows(p), cols])
            grad_scores = weights * (grad_weights - joint[p, pl.ds(HEADS + h, 1), :])
            grad_low = grad_scores.astype(BF16)
            wl[h, :, pair_rows(p)] = weights.astype(BF16)
            gl[h, :, pair_rows(p)] = grad_low
            grad_query = (nn(kt[h], grad_low) * SCALING).T
            gqb[p, :, :, cols] = grad_query.reshape(PLANE, UNIT, DH).astype(BF16)
            return carry

        lax.fori_loop(0, HEADS, one, 0)
        plane_all(gqb.at[p], gr.at[p], gr_send.at[p], gr_recv.at[p])

    def arrived(p):
        await_bytes(gr.at[p, pl.ds(0, PLANE - 1)], gr_recv.at[p])

    def span_sums(i, lo, n):
        p, side = i // 2, i % 2
        row, lane = iota((n, PAIR_ROWS), 0) + lo, iota((n, PAIR_ROWS), 1)
        hit = (tabz[i, 0:1, TAB_A:TAB_B] == row // SPAN) & (lane % UNIT == row % SPAN + SPAN * side)
        return nn(jnp.where(hit, 1.0, 0.0).astype(BF16), gr[p].reshape(PAIR_ROWS, FEATS))

    homes = {}

    def home(step):
        for part in range(2):
            for direction in range(2):
                if step == 1 and part != direction:
                    continue
                rows = pl.ds(part * half, half)
                i = FAR if step == 1 else 2 * (4 - step) + 1 - direction
                sums = span_sums(i, part * half, half)
                if (direction, step - 1, part) in homes:
                    homes[direction, step - 1, part].wait_recv()
                    sums += rs_in[direction, step - 2, rows, :].astype(F32)
                rs_out[direction, step - 1, rows, :] = sums.astype(BF16)
                copy = remote(
                    rs_out.at[direction, step - 1, rows, :], rs_in.at[direction, step - 1, rows, :],
                    rs_send.at[direction, step - 1, part], rs_recv.at[direction, step - 1, part],
                    z_peer(1 if direction == 0 else -1),
                )
                copy.start()
                homes[direction, step, part] = copy

    def cache_grads(h, carry):
        cols = head_cols(h)
        gck[:, cols] = (nn(gl[h], qs[:, cols]) * SCALING).astype(BF16)
        gcv[:, cols] = nn(wl[h], gs[:, cols]).astype(BF16)
        return carry

    second(3)
    second(2)
    arrived(3)
    home(1)
    second(1)
    arrived(2)
    home(2)
    second(0)
    arrived(1)
    home(3)
    lax.fori_loop(0, HEADS // 2, cache_grads, 0)
    arrived(0)
    home(4)
    lax.fori_loop(HEADS // 2, HEADS, cache_grads, 0)
    store_k = pltpu.make_async_copy(gck, gck_hbm, local_sem.at[5])
    store_v = pltpu.make_async_copy(gcv, gcv_hbm, local_sem.at[6])
    store_k.start()
    store_v.start()
    for part in range(2):
        rows = pl.ds(part * half, half)
        sums = own_gq[rows, :] + span_sums(OWN, part * half, half)
        for direction in range(2):
            homes[direction, 4, part].wait_recv()
            sums += rs_in[direction, 3, rows, :].astype(F32)
        gq_out[rows, :] = sums.astype(BF16)

    for swap in swaps:
        swap.wait_send()
    for copy in tabs + stats_home + norms_out + list(rings.values()) + list(homes.values()):
        copy.wait_send()
    for i in range(NZ):
        await_bytes(sbuf.at[i], plane_send.at[i])
    await_bytes(st_out.at[pl.ds(0, PLANE - 1)], st_send.at[0])
    await_bytes(nr_out.at[pl.ds(0, PLANE - 1)], nr_send.at[0])
    for p in range(PAIRS):
        await_bytes(gqb.at[p, pl.ds(0, PLANE - 1)], gr_send.at[p])
    store_k.wait()
    store_v.wait()


def run_kernel(queries, grad_out, new_keys, new_values, cache_keys, cache_values, table, picks):
    vmem = pl.BlockSpec(memory_space=pltpu.VMEM)
    hbm = pl.BlockSpec(memory_space=pl.ANY)
    rows = jax.ShapeDtypeStruct((ROWS, FEATS), BF16)
    block = jax.ShapeDtypeStruct((BLK, FEATS), BF16)
    dma = pltpu.SemaphoreType.DMA
    units = (PLANE, UNIT, FEATS)
    return pl.pallas_call(
        kernel,
        out_shape=(rows, rows, rows, block, block),
        in_specs=[hbm] * 6 + [vmem] * 2,
        out_specs=(vmem, vmem, vmem, hbm, hbm),
        scratch_shapes=[
            *[pltpu.VMEM((ROWS, FEATS), BF16)] * 4,
            *[pltpu.VMEM((BLK, FEATS), BF16)] * 2,
            pltpu.VMEM((HEADS, DH, BLK), BF16),
            [pltpu.VMEM((SPANS + 1, UNIT, FEATS), BF16)] * NZ,
            pltpu.VMEM((NZ, PLANE - 1, UNIT, FEATS), BF16),
            pltpu.VMEM((NZ,) + units, BF16),
            pltpu.VMEM((NZ, SPAN, TAB_END), jnp.int32),
            pltpu.SMEM((NZ, SPAN, TAB_END - TAB_S), jnp.int32),
            *[pltpu.VMEM((PAIRS * PAIR_ROWS, FEATS), BF16)] * 2,
            *[pltpu.VMEM((HEADS, BLK, PAIRS * PAIR_ROWS), BF16)] * 2,
            pltpu.VMEM((PAIRS, 2 * HEADS, PAIR_ROWS), F32),
            pltpu.VMEM((2 * HEADS, ROWS), F32),
            *[pltpu.VMEM((PLANE, NZ, 128), F32)] * 2,
            *[pltpu.VMEM((NZ, PLANE, 128), F32)] * 2,
            pltpu.VMEM((NZ, SPANS, 128), F32),
            *[pltpu.VMEM((PLANE, NZ, 128), F32)] * 2,
            pltpu.VMEM((PAIRS, 2 * HEADS, PAIR_ROWS), F32),
            pltpu.VMEM((2 * HEADS, ROWS), F32),
            *[pltpu.VMEM((PAIRS,) + units, BF16)] * 2,
            *[pltpu.VMEM((2, 4, ROWS, FEATS), BF16)] * 2,
            pltpu.VMEM((ROWS, FEATS), F32),
            *[pltpu.VMEM((BLK, FEATS), BF16)] * 2,
            dma((4,)), dma((4,)), dma((7,)),
            dma((NZ,)), dma((NZ,)),
            dma((2, 4, CHUNKS)), dma((2, 4, CHUNKS)),
            dma((NZ,)), dma((NZ,)),
            dma((1,)), dma((1,)), dma((NZ,)), dma((NZ,)),
            dma((NZ,)), dma((NZ,)), dma((1,)), dma((1,)),
            dma((PAIRS,)), dma((PAIRS,)),
            dma((2, 4, 2)), dma((2, 4, 2)),
        ],
        compiler_params=pltpu.CompilerParams(
            collective_id=0, has_side_effects=True, vmem_limit_bytes=60 * 1024 * 1024
        ),
    )(queries, grad_out, new_keys, new_values, cache_keys, cache_values, table, picks)


def body(queries, new_keys, new_values, grad_out, cache_keys, cache_values, choices):
    z = lax.axis_index("seq") // PLANE
    lanes = jnp.concatenate(
        [
            jnp.arange(256, dtype=jnp.int32) // UNIT,
            jnp.arange(128, dtype=jnp.int32) // NZ,
            jnp.arange(128, dtype=jnp.int32) % PLANE,
        ]
    )
    blocks = jnp.arange(NZ, dtype=jnp.int32)[:, None] * PLANE + lanes[None, :]
    hits = choices[:, :, None, None] == blocks[None, None]
    spans = jnp.arange(SPANS, dtype=jnp.int32)[:, None, None, None]
    table = jnp.min(jnp.where(hits, spans, SPANS), axis=(0, 1))
    table = jnp.broadcast_to(table[:, None, :], (NZ, SPAN, TAB_END))
    away = (choices // PLANE - z) % NZ
    group = jnp.where(away == 0, OWN, jnp.where(away < 4, 2 * away - 1, 14 - 2 * away))
    group = jnp.where(away == 4, FAR, group)
    picks = (group * PLANE + choices % PLANE).T.reshape(TOPK * SPANS, 1)
    picks = jnp.broadcast_to(picks, (TOPK * SPANS, 128))
    return run_kernel(
        queries, grad_out, new_keys, new_values, cache_keys, cache_values, table, picks
    )


def solution(mesh):
    rows = P(("seq", "head"), None)
    both = P("seq", "head")
    return jax.shard_map(
        body,
        mesh=mesh,
        in_specs=(rows, rows, rows, rows, both, both, P("seq", None)),
        out_specs=(both,) * 5,
        check_vma=False,
    )
```

time: 258 us -> 152 us (0.59)
  Pallas kernels: 69.8 us -> 140 us
  matrix products: 44.2 us -> 0 us
  local copies, waits for them, and re-layouts: 52.8 us -> 9.84 us
  waiting for transfers between devices: 40.5 us -> 0 us
  other arithmetic: 25.6 us -> 0.28 us
  starting transfers between devices: 23.5 us -> 0 us
    pallas_call x1, Pallas kernels: 69.8 us -> 140 us  [run_kernel(): pl.pallas_call(kernel, out_shape=(rows, rows, rows, block, block), in_spe...]
    dot_general x10 -> x0, matrix products: 44.2 us -> none  [the longest x1 11.3 us: block_stats(): jnp.einsum('rhd,khd->hrk', grad_tile, value_rows, preferred_element_type=...]
    all_to_all x3 -> x0, waiting for transfers between devices: 40.5 us -> none  [exchange(): return lax.all_to_all(slots, 'seq', split_axis=0, concat_axis=0, tiled=True)]
    all_to_all x3 -> x0, starting transfers between devices: 23.5 us -> none  [exchange(): return lax.all_to_all(slots, 'seq', split_axis=0, concat_axis=0, tiled=True)]
    gather x10 -> x0, local copies, waits for them, and re-layouts: 14.5 us -> none  [the longest x6 9.51 us: regroup(): return jnp.take(slots.reshape(NZ, -1), order, axis=0).reshape(slots.shape)]
    convert_element_type x3 -> x0, other arithmetic: 12.2 us -> none  [the longest x2 12.1 us: block_grads(): grad_low = grad_scores.astype(jnp.bfloat16)]
    unnamed x60 -> x12, local copies, waits for them, and re-layouts: 19.2 us -> 8.41 us
    reshape x13 -> x0, local copies, waits for them, and re-layouts: 9.88 us -> none  [the longest x1 4.15 us: body(): work_grad = received[:, :, SPAN:].reshape(devices * SPAN, HEADS, DH)]
  transfers between devices with their start and end apart: 3 -> 0, of which waited for: 3 -> 0; matrix products, arithmetic and copies ran while one was open for 13% -> 0% of each run, Pallas kernels for 0% -> 0%
where the time goes in v2:
time: 152 us; the launch traced here: 151 us
  Pallas kernels  140 us (92%)
  local copies, waits for them, and re-layouts  9.84 us (6%)
    pallas_call x1, Pallas kernels, run_kernel(): pl.pallas_call(kernel, out_shape=(rows, rows, rows, block, block), in_spe...  140 us
    unnamed x12, local copies, waits for them, and re-layouts  8.41 us

profile of v2, /device:TPU:32, one launch (start us, length us, event | category | flops | bytes accessed | tf_op | source)
XLA Modules:
  0.0 150.9 jit_solution(4651202215043697689)
XLA Ops:
  0.7 0.0 copy-start.2
  0.7 0.7 copy-done.2
  1.4 0.1 broadcast_in_dim.39
  1.5 0.1 copy.13
  1.6 0.1 broadcast_add_fusion
  1.6 0.2 select_reduce_fusion
  1.8 0.7 broadcast_in_dim.40.sel_ref
  2.5 0.7 broadcast_in_dim.37.tab_ref
  3.1 140.1 %shard_map.110 = (bf16[128,1024]{1,0:T(8,128)(2,1)}, bf16[128,1024]{1,0:T(8,128)(2,1)}, bf16[128,1024]{1,0:T(8,128)(2,1)}, bf16[512,1024]{1,0:T(8,128)(2,1)}, bf16[512,1024]{1,0:T(8,128)(2,1)}) custom-call(bf16[64,2048]{1,0:T(8,128)(2,1)} %q_hbm.1, bf16[64,2048]{1,0:T(8,128)(2,1)} %g_hbm.1, bf16[64,2048]{1,0:T(8,128)(2,1)} %k_hbm.1, bf16[64,2048]{1,0:T(8,128)(2,1)} %v_hbm.1, ...), custom_call_target="tpu_custom_call" | custom-call | tf_op jit(solution)/shard_map/pallas_call | solution.py:497
  143.3 0.0 copy-start.1
  143.3 1.8 %copy.19 = bf16[128,1024]{1,0:T(8,128)(2,1)} copy(bf16[128,1024]{1,0:T(8,128)(2,1)} %get-tuple-element.12) | data formatting | bytes 524288
  145.0 1.7 %copy.20 = bf16[128,1024]{1,0:T(8,128)(2,1)} copy(bf16[128,1024]{1,0:T(8,128)(2,1)} %get-tuple-element.13) | data formatting | bytes 524288
  146.7 1.7 %copy.21 = bf16[128,1024]{1,0:T(8,128)(2,1)} copy(bf16[128,1024]{1,0:T(8,128)(2,1)} %get-tuple-element.14) | data formatting | bytes 524288
  148.4 0.0 copy-done.1
  148.4 0.0 copy-start
  148.4 1.0 copy.22
  149.3 0.6 copy-done
  150.0 1.0 copy.23
  (5 shorter events, 0.0 us)
Async XLA Ops:
  0.7 0.7 copy-start.2
  143.3 5.1 %copy-start.1 = (bf16[512,1024]{1,0:T(8,128)(2,1)S(1)}, bf16[512,1024]{1,0:T(8,128)(2,1)}, u32[]{:S(2)}) copy-start(bf16[512,1024]{1,0:T(8,128)(2,1)} %get-tuple-element.15) | copy-start | bytes 3145732
  148.4 1.6 %copy-start = (bf16[512,1024]{1,0:T(8,128)(2,1)S(1)}, bf16[512,1024]{1,0:T(8,128)(2,1)}, u32[]{:S(2)}) copy-start(bf16[512,1024]{1,0:T(8,128)(2,1)} %get-tuple-element.16) | copy-start | bytes 3145732

commit v3 on v2

v3 whole, which is shorter than its diff:
```python
import math

import jax
import jax.numpy as jnp
from jax import lax
from jax.experimental import pallas as pl
from jax.experimental.pallas import tpu as pltpu
from jax.sharding import PartitionSpec as P

DH = 128
SPAN = 8
TOPK = 3
NZ = 8
NX = 4
NY = 4
PLANE = NX * NY
SPANS = 16
FEATS = 1024
HEADS = FEATS // DH
ROWS = SPANS * SPAN
BLK = 512
PAIRS = NZ // 2
PAIR_ROWS = 2 * PLANE * SPAN
UNIT = 2 * SPAN
CHUNKS = 4
NC = 2
WIDTH = FEATS // NC
HALF = HEADS // NC
CHUNK = SPANS // CHUNKS
SCALING = 1.0 / math.sqrt(DH)
LOG2E = math.log2(math.e)
SCALING2 = SCALING * LOG2E
MESH = pl.DeviceIdType.MESH
OFFSETS = (-1, 1, -2, 2, -3, 3, 0, 4)
GROUP_OF = (6, 1, 3, 5, 7, 4, 2, 0)
OWN = 6
FAR = 7
TAB_A, TAB_B, TAB_S, TAB_END = 0, 256, 384, 512
BF16 = jnp.bfloat16
F32 = jnp.float32
HIGHEST = lax.Precision.HIGHEST


def iota(shape, axis):
    return lax.broadcasted_iota(jnp.int32, shape, axis)


def nt(a, b, precision=None):
    return lax.dot_general(
        a, b, (((1,), (1,)), ((), ())), precision=precision, preferred_element_type=F32
    )


def tn(a, b, precision=None):
    return lax.dot_general(
        a, b, (((0,), (0,)), ((), ())), precision=precision, preferred_element_type=F32
    )


def nn(a, b, precision=None):
    return jnp.dot(a, b, precision=precision, preferred_element_type=F32)


def lane_mask(lanes):
    return iota((128, lanes), 0) // 16 == iota((128, lanes), 1) % SPAN


def pick_pair(p):
    row, lane = iota((128, PAIR_ROWS), 0), iota((128, PAIR_ROWS), 1)
    hit = (row // NZ == lane // UNIT) & (row % NZ == 2 * p + (lane // SPAN) % 2)
    return hit.astype(F32)


def pick_own():
    return (iota((SPANS, ROWS), 0) == iota((SPANS, ROWS), 1) // SPAN).astype(F32)


def stacked(stats):
    tall = jnp.concatenate([stats] * SPAN, axis=0)
    return jnp.where(lane_mask(stats.shape[1]), tall, 0.0)


def unstacked(wide):
    kept = jnp.where(lane_mask(wide.shape[1]), wide, 0.0)
    return jnp.sum(kept.reshape(SPAN, 2 * HEADS, wide.shape[1]), axis=0)


def head_cols(h):
    return pl.ds(pl.multiple_of(h * DH, DH), DH)


def kernel(
    q_hbm, g_hbm, k_hbm, v_hbm, ck_hbm, cv_hbm, tab_ref, sel_ref,
    gq_hbm, gnk_hbm, gnv_hbm, gck_hbm, gcv_hbm,
    own_q, own_g, own_k, own_v, kc, vc, kt,
    zbufs, sbuf, rbuf, tabz, tab_smem, qs, gs, wl, gl,
    stat, own_stat, st_out, st_in, zst_out, zst_in, nz, nr_out, nr_in, joint, own_joint,
    gqb, gr, rs_out, rs_in, own_gq, gq, gnk, gnv, gck, gcv,
    head_send, head_recv, local_sem, tab_send, tab_recv, ring_send, ring_recv,
    plane_send, plane_recv, st_send, st_recv, zst_send, zst_recv, nz_send, nz_recv,
    nr_send, nr_recv, gr_send, gr_recv, rs_send, rs_recv,
):
    seq = lax.axis_index("seq")
    head = lax.axis_index("head")
    z = seq // PLANE
    t0 = seq % PLANE
    x0 = t0 // NY
    y0 = t0 % NY

    def z_peer(d):
        return (((z + d) % NZ) * PLANE + t0, head)

    def plane_of(o):
        m = (5 * o) % PLANE
        return ((x0 + m // NY) % NX) * NY + (y0 + m % NY) % NY

    def plane_peer(t):
        return (z * PLANE + t, head)

    def remote(src, dst, send, recv, device):
        return pltpu.make_async_remote_copy(
            src_ref=src, dst_ref=dst, send_sem=send, recv_sem=recv,
            device_id=device, device_id_type=MESH,
        )

    def await_bytes(ref, sem):
        pltpu.make_async_copy(ref, ref, sem).wait()

    half = ROWS // 2
    my_rows = pl.ds(pl.multiple_of(head * half, half), half)
    my_cols = pl.ds(pl.multiple_of(head * FEATS, FEATS), FEATS)
    other_cols = pl.ds(pl.multiple_of((1 - head) * FEATS, FEATS), FEATS)
    sources = ((q_hbm, own_q), (g_hbm, own_g), (k_hbm, own_k), (v_hbm, own_v))
    keeps = [
        pltpu.make_async_copy(src.at[:, my_cols], dst.at[my_rows, :], local_sem.at[i])
        for i, (src, dst) in enumerate(sources)
    ]
    for keep in keeps:
        keep.start()
    fetch_k = pltpu.make_async_copy(ck_hbm, kc, local_sem.at[5])
    fetch_v = pltpu.make_async_copy(cv_hbm, vc, local_sem.at[6])
    fetch_k.start()
    fetch_v.start()

    sibling = (seq, 1 - head)
    barrier = pltpu.get_barrier_semaphore()
    pl.semaphore_signal(barrier, inc=1, device_id=sibling, device_id_type=MESH)
    for d in range(1, NZ):
        pl.semaphore_signal(barrier, inc=1, device_id=z_peer(d), device_id_type=MESH)

    def greet(o, carry):
        pl.semaphore_signal(
            barrier, inc=1, device_id=plane_peer(plane_of(o)), device_id_type=MESH
        )
        return carry

    lax.fori_loop(1, PLANE, greet, 0)
    for c in range(NC):
        for i in range(NZ):
            zbufs[c][i][SPANS] = jnp.zeros((UNIT, WIDTH), BF16)
    stat[...] = jnp.zeros(stat.shape, F32)
    own_stat[...] = jnp.zeros(own_stat.shape, F32)
    tabz[OWN] = tab_ref[z]
    pl.semaphore_wait(barrier, 1 + (NZ - 1) + (PLANE - 1))

    swaps = [
        remote(src.at[:, other_cols], dst.at[my_rows, :], head_send.at[i], head_recv.at[i], sibling)
        for i, (src, dst) in enumerate(sources)
    ]
    for swap in swaps[:2]:
        swap.start()
    tabs = []
    for d in range(1, NZ):
        i = GROUP_OF[(-d) % NZ]
        tab = remote(tab_ref.at[(z + d) % NZ], tabz.at[i], tab_send.at[d], tab_recv.at[i], z_peer(d))
        tab.start()
        tabs.append(tab)
    for swap in swaps[2:]:
        swap.start()
    for i in (0, 1):
        keeps[i].wait()
        swaps[i].wait_recv()

    def half_cols(c):
        return pl.ds(c * WIDTH, WIDTH)

    def pack(c):
        def one(i, carry):
            rows = pl.ds(pl.multiple_of(UNIT * i, UNIT), UNIT)
            qpair = own_q[rows, half_cols(c)].astype(F32)
            gpair = own_g[rows, half_cols(c)].astype(F32)
            zbufs[c][OWN][2 * i] = jnp.concatenate([qpair[:SPAN], gpair[:SPAN]], axis=0).astype(BF16)
            zbufs[c][OWN][2 * i + 1] = jnp.concatenate([qpair[SPAN:], gpair[SPAN:]], axis=0).astype(
                BF16
            )
            return carry

        return one

    rings = {}

    def ring(c, direction, step, chunk):
        src_i = OWN if step == 1 else 2 * (step - 2) + direction
        dst_i = FAR if step == 4 else 2 * (step - 1) + direction
        part = pl.ds(chunk * CHUNK, CHUNK)
        copy = remote(
            zbufs[c][src_i].at[part], zbufs[c][dst_i].at[part],
            ring_send.at[c, direction, step - 1, chunk],
            ring_recv.at[c, direction, step - 1, chunk],
            z_peer(1 if direction == 0 else -1),
        )
        copy.start()
        rings[c, direction, step, chunk] = copy

    for chunk in range(CHUNKS):
        lax.fori_loop(2 * chunk, 2 * chunk + 2, pack(0), 0)
        for direction in range(2):
            ring(0, direction, 1, chunk)

    for tab in tabs:
        tab.wait_recv()
    to_smem = pltpu.make_async_copy(
        tabz.at[:, :, pl.ds(TAB_S, TAB_END - TAB_S)], tab_smem, local_sem.at[4]
    )
    to_smem.start()
    to_smem.wait()

    def spread(c, i):
        def one(o, carry):
            t = plane_of(o)
            sbuf[c, i, o - 1] = zbufs[c][i][tab_smem[i, 0, t]]
            remote(
                sbuf.at[c, i, o - 1], rbuf.at[c, i, t0],
                plane_send.at[c, i], plane_recv.at[c, i], plane_peer(t),
            ).start()
            return carry

        lax.fori_loop(1, PLANE, one, 0)
        rbuf[c, i, t0] = zbufs[c][i][tab_smem[i, 0, t0]]

    def pair_rows(p):
        return pl.ds(p * PAIR_ROWS, PAIR_ROWS)

    def first(c, p):
        for i in (2 * p, 2 * p + 1):
            await_bytes(rbuf.at[c, i, pl.ds(0, PLANE - 1)], plane_recv.at[c, i])

        def unpack(t, carry):
            rows = pl.ds(pl.multiple_of(p * PAIR_ROWS + t * UNIT, UNIT), UNIT)
            a = rbuf[c, 2 * p, t].astype(F32)
            b = rbuf[c, 2 * p + 1, t].astype(F32)
            qs[rows, half_cols(c)] = jnp.concatenate([a[:SPAN], b[:SPAN]], axis=0).astype(BF16)
            gs[rows, half_cols(c)] = jnp.concatenate([a[SPAN:], b[SPAN:]], axis=0).astype(BF16)
            return carry

        lax.fori_loop(0, PLANE, unpack, 0)

        def one(k, carry):
            cols = head_cols(HALF * c + k)
            scores = nt(kc[:, cols], qs[pair_rows(p), cols]) * SCALING2
            high = jnp.max(scores, axis=0, keepdims=True)
            weights = jnp.exp2(scores - high)
            total = jnp.sum(weights, axis=0, keepdims=True)
            grad_weights = nt(vc[:, cols], gs[pair_rows(p), cols])
            inner = jnp.sum(weights * grad_weights, axis=0, keepdims=True)
            stat[c, p, pl.ds(k, 1), :] = high + jnp.log(total) * LOG2E
            stat[c, p, pl.ds(HEADS + k, 1), :] = inner / total
            return carry

        lax.fori_loop(0, HALF, one, 0, unroll=HALF)

    def own_scores(cols):
        scores = nt(own_k[:, cols], own_q[:, cols]) * SCALING2
        seen = iota((ROWS, ROWS), 0) <= iota((ROWS, ROWS), 1)
        return jnp.where(seen, scores, -jnp.inf)

    def own_first(c):
        def one(k, carry):
            cols = head_cols(HALF * c + k)
            scores = own_scores(cols)
            high = jnp.max(scores, axis=0, keepdims=True)
            weights = jnp.exp2(scores - high)
            total = jnp.sum(weights, axis=0, keepdims=True)
            grad_weights = nt(own_v[:, cols], own_g[:, cols])
            inner = jnp.sum(weights * grad_weights, axis=0, keepdims=True)
            own_stat[c, pl.ds(k, 1), :] = high + jnp.log(total) * LOG2E
            own_stat[c, pl.ds(HEADS + k, 1), :] = inner / total
            return carry

        return one

    def turn_keys(h, carry):
        kt[h] = kc[:, head_cols(h)].T
        return carry

    def ring_step(c, step, work):
        for chunk in range(CHUNKS):
            for direction in range(2):
                if step == 4 and chunk // 2 != direction:
                    continue
                rings[c, direction, step, chunk].wait_recv()
                if step < 3 or (step == 3 and chunk // 2 == direction):
                    ring(c, direction, step + 1, chunk)
            work(chunk)
        if step < 4:
            spread(c, 2 * (step - 1))
            spread(c, 2 * (step - 1) + 1)
        else:
            spread(c, FAR)

    def plane_all(out, into, send, recv):
        def one(o, carry):
            t = plane_of(o)
            remote(out.at[t], into.at[t0], send, recv, plane_peer(t)).start()
            return carry

        lax.fori_loop(1, PLANE, one, 0)
        into[t0] = out[t0]

    small = []

    def stats_plane(c):
        slots = nt(pick_pair(0), stacked(stat[c, 0]), HIGHEST)
        for p in range(1, PAIRS):
            slots += nt(pick_pair(p), stacked(stat[c, p]), HIGHEST)
        st_out[c] = slots.reshape(PLANE, NZ, 128)
        plane_all(st_out.at[c], st_in.at[c], st_send.at[c], st_recv.at[c])

    stats_home = {}

    def stats_z(c):
        row, lane = iota((128, 128), 0), iota((128, 128), 1)
        swap_order = ((row // PLANE == lane % NZ) & (row % PLANE == lane // NZ)).astype(F32)
        await_bytes(st_in.at[c, pl.ds(0, PLANE - 1)], st_recv.at[c])
        zst_out[c] = nn(swap_order, st_in[c].reshape(128, 128), HIGHEST).reshape(NZ, PLANE, 128)
        stats_home[c] = []
        for i in range(NZ):
            j = GROUP_OF[(-OFFSETS[i]) % NZ]
            if i == OWN:
                zst_in[c, OWN] = zst_out[c, OWN]
                continue
            copy = remote(
                zst_out.at[c, i], zst_in.at[c, j], zst_send.at[c, i], zst_recv.at[c, j],
                z_peer(OFFSETS[i]),
            )
            copy.start()
            stats_home[c].append(copy)
            small.append(copy)

    norms_out = {}

    def norms_z(c):
        own_slots = nt(pick_own(), stacked(own_stat[c]), HIGHEST)
        chosen = (sel_ref[...] == iota((TOPK * SPANS, 128), 1)).astype(F32)
        for copy in stats_home[c]:
            copy.wait_recv()
        picked = nn(chosen, zst_in[c].reshape(128, 128), HIGHEST)
        logs = [own_slots] + [picked[SPANS * t:SPANS * (t + 1)] for t in range(TOPK)]
        peak = jnp.maximum(jnp.maximum(logs[0], logs[1]), jnp.maximum(logs[2], logs[3]))
        shares = [jnp.exp2(log - peak) for log in logs]
        total = (shares[0] + shares[1]) + (shares[2] + shares[3])
        norm = peak + jnp.log(total) * LOG2E
        delta = jnp.zeros((SPANS, 128), F32)
        for share, log in zip(shares, logs):
            delta += pltpu.roll(share / total, HEADS, 1) * log
        is_norm = iota((SPANS, 128), 1) % (2 * HEADS) < HEADS
        nz[c, OWN] = jnp.where(is_norm, norm, delta)
        norms_out[c] = []
        for d in range(1, NZ):
            i = GROUP_OF[(-d) % NZ]
            copy = remote(
                nz.at[c, OWN], nz.at[c, i], nz_send.at[c, d], nz_recv.at[c, i], z_peer(d)
            )
            copy.start()
            norms_out[c].append(copy)
            small.append(copy)
        own_joint[c] = unstacked(tn(nz[c, OWN], pick_own(), HIGHEST))

    def norms_plane(c):
        lane8 = iota((SPANS, 128), 1) % NZ
        span_row = iota((SPANS, 128), 0)
        routes = jnp.concatenate(
            [
                jnp.where((lane8 == i) & (tabz[i, 0:1, TAB_B:TAB_S] == span_row), 1.0, 0.0)
                for i in range(NZ)
            ],
            axis=0,
        ).astype(F32)
        for copy in norms_out[c]:
            copy.wait_recv()
        routed = tn(routes, nz[c].reshape(128, 128), HIGHEST)
        nr_out[c] = routed.reshape(PLANE, NZ, 128)
        plane_all(nr_out.at[c], nr_in.at[c], nr_send.at[c], nr_recv.at[c])

    def norms_arrived(c):
        await_bytes(nr_in.at[c, pl.ds(0, PLANE - 1)], nr_recv.at[c])

    def own_second(c):
        def one(k, carry):
            cols = head_cols(HALF * c + k)
            weights = jnp.exp2(own_scores(cols) - own_joint[c, pl.ds(k, 1), :])
            grad_weights = nt(own_v[:, cols], own_g[:, cols])
            grad_scores = weights * (grad_weights - own_joint[c, pl.ds(HEADS + k, 1), :])
            weights_low = weights.astype(BF16)
            grad_low = grad_scores.astype(BF16)
            own_gq[:, cols] = tn(grad_low, own_k[:, cols]) * SCALING
            gnk[:, cols] = (nn(grad_low, own_q[:, cols]) * SCALING).astype(BF16)
            gnv[:, cols] = nn(weights_low, own_g[:, cols]).astype(BF16)
            return carry

        lax.fori_loop(0, HALF, one, 0, unroll=2)

    def second(c, p):
        joint[c, p] = unstacked(tn(nr_in[c].reshape(128, 128), pick_pair(p), HIGHEST))

        def one(k, carry):
            h = HALF * c + k
            cols = head_cols(h)
            scores = nt(kc[:, cols], qs[pair_rows(p), cols]) * SCALING2
            weights = jnp.exp2(scores - joint[c, p, pl.ds(k, 1), :])
            grad_weights = nt(vc[:, cols], gs[pair_rows(p), cols])
            grad_scores = weights * (grad_weights - joint[c, p, pl.ds(HEADS + k, 1), :])
            grad_low = grad_scores.astype(BF16)
            wl[h, :, pair_rows(p)] = weights.astype(BF16)
            gl[h, :, pair_rows(p)] = grad_low
            grad_query = (nn(kt[h], grad_low) * SCALING).T
            gqb[c, p, :, :, head_cols(k)] = grad_query.reshape(PLANE, UNIT, DH).astype(BF16)
            return carry

        lax.fori_loop(0, HALF, one, 0, unroll=HALF)
        plane_all(gqb.at[c, p], gr.at[c, p], gr_send.at[c, p], gr_recv.at[c, p])

    def arrived(c, p):
        await_bytes(gr.at[c, p, pl.ds(0, PLANE - 1)], gr_recv.at[c, p])

    def span_sums(c, i, lo, n):
        p, side = i // 2, i % 2
        row, lane = iota((n, PAIR_ROWS), 0) + lo, iota((n, PAIR_ROWS), 1)
        hit = (tabz[i, 0:1, TAB_A:TAB_B] == row // SPAN) & (lane % UNIT == row % SPAN + SPAN * side)
        return nn(jnp.where(hit, 1.0, 0.0).astype(BF16), gr[c, p].reshape(PAIR_ROWS, WIDTH))

    homes = {}

    def home(c, step):
        arrived(c, 4 - step)
        for direction in range(2):
            lo, n = (direction * half, half) if step == 1 else (0, ROWS)
            rows = pl.ds(lo, n)
            i = FAR if step == 1 else 2 * (4 - step) + 1 - direction
            sums = span_sums(c, i, lo, n)
            if step == 1:
                rs_out[c, direction, 0, rows, :] = sums.astype(BF16)
            else:
                homes[c, direction, step - 1].wait_recv()
                came = pl.ds(direction * half, half) if step == 2 else rows
                rs_out[c, direction, step - 1] = sums.astype(BF16)
                if step == 2:
                    part = sums[direction * half:(direction + 1) * half]
                else:
                    part = sums
                part += rs_in[c, direction, step - 2, came, :].astype(F32)
                rs_out[c, direction, step - 1, came, :] = part.astype(BF16)
            copy = remote(
                rs_out.at[c, direction, step - 1, rows, :],
                rs_in.at[c, direction, step - 1, rows, :],
                rs_send.at[c, direction, step - 1], rs_recv.at[c, direction, step - 1],
                z_peer(1 if direction == 0 else -1),
            )
            copy.start()
            homes[c, direction, step] = copy

    def cache_grads(c):
        def one(k, carry):
            h = HALF * c + k
            cols = head_cols(h)
            gck[:, cols] = (nn(gl[h], qs[:, cols]) * SCALING).astype(BF16)
            gcv[:, cols] = nn(wl[h], gs[:, cols]).astype(BF16)
            return carry

        lax.fori_loop(0, HALF, one, 0, unroll=2)

    def finish(c):
        sums = own_gq[:, half_cols(c)] + span_sums(c, OWN, 0, ROWS)
        for direction in range(2):
            homes[c, direction, 4].wait_recv()
            sums += rs_in[c, direction, 3].astype(F32)
        gq[:, half_cols(c)] = sums.astype(BF16)

    def nothing(chunk):
        pass

    def own_work(chunk):
        lax.fori_loop(2 * (chunk % 2), 2 * (chunk % 2) + 2, own_first(chunk // 2), 0)

    def turn_work(chunk):
        lax.fori_loop(2 * chunk, 2 * chunk + 2, turn_keys, 0)

    def next_half(chunk):
        lax.fori_loop(2 * chunk, 2 * chunk + 2, pack(1), 0)
        for direction in range(2):
            ring(1, direction, 1, chunk)

    spread(0, OWN)
    for i in (2, 3):
        keeps[i].wait()
        swaps[i].wait_recv()
    fetch_k.wait()
    fetch_v.wait()
    ring_step(0, 1, own_work)
    ring_step(0, 2, turn_work)
    ring_step(0, 3, next_half)
    spread(1, OWN)
    ring_step(0, 4, nothing)
    first(0, 0)
    ring_step(1, 1, nothing)
    first(0, 1)
    ring_step(1, 2, nothing)
    first(0, 2)
    first(0, 3)
    stats_plane(0)
    ring_step(1, 3, nothing)
    stats_z(0)
    ring_step(1, 4, nothing)
    norms_z(0)
    first(1, 0)
    first(1, 1)
    norms_plane(0)
    first(1, 2)
    first(1, 3)
    stats_plane(1)
    norms_arrived(0)
    second(0, 3)
    second(0, 2)
    stats_z(1)
    second(0, 1)
    second(0, 0)
    norms_z(1)
    home(0, 1)
    own_second(0)
    norms_plane(1)
    home(0, 2)
    norms_arrived(1)
    second(1, 3)
    second(1, 2)
    home(0, 3)
    second(1, 1)
    second(1, 0)
    home(0, 4)
    own_second(1)
    store_nk = pltpu.make_async_copy(gnk, gnk_hbm, local_sem.at[0])
    store_nv = pltpu.make_async_copy(gnv, gnv_hbm, local_sem.at[1])
    store_nk.start()
    store_nv.start()
    home(1, 1)
    cache_grads(0)
    home(1, 2)
    cache_grads(1)
    store_k = pltpu.make_async_copy(gck, gck_hbm, local_sem.at[5])
    store_v = pltpu.make_async_copy(gcv, gcv_hbm, local_sem.at[6])
    store_k.start()
    store_v.start()
    home(1, 3)
    home(1, 4)
    finish(0)
    finish(1)
    store_q = pltpu.make_async_copy(gq, gq_hbm, local_sem.at[2])
    store_q.start()

    for copy in swaps + tabs + small + list(rings.values()) + list(homes.values()):
        copy.wait_send()
    for c in range(NC):
        for i in range(NZ):
            await_bytes(sbuf.at[c, i], plane_send.at[c, i])
        await_bytes(st_out.at[c, pl.ds(0, PLANE - 1)], st_send.at[c])
        await_bytes(nr_out.at[c, pl.ds(0, PLANE - 1)], nr_send.at[c])
        for p in range(PAIRS):
            await_bytes(gqb.at[c, p, pl.ds(0, PLANE - 1)], gr_send.at[c, p])
    for store in (store_nk, store_nv, store_k, store_v, store_q):
        store.wait()


def hand_over(*refs):
    made, results, held, (sems,) = refs[:5], refs[5:10], refs[10:15], refs[15:]
    loads = [pltpu.make_async_copy(made[i], held[i], sems.at[0, i]) for i in range(5)]
    stores = [pltpu.make_async_copy(held[i], results[i], sems.at[1, i]) for i in range(5)]
    for load in loads:
        load.start()
    for load, store in zip(loads, stores):
        load.wait()
        store.start()
    for store in stores:
        store.wait()


def run_kernel(queries, grad_out, new_keys, new_values, cache_keys, cache_values, table, picks):
    vmem = pl.BlockSpec(memory_space=pltpu.VMEM)
    hbm = pl.BlockSpec(memory_space=pl.ANY)
    rows = jax.ShapeDtypeStruct((ROWS, FEATS), BF16)
    block = jax.ShapeDtypeStruct((BLK, FEATS), BF16)
    results = (rows, rows, rows, block, block)
    dma = pltpu.SemaphoreType.DMA
    units = (PLANE, UNIT, WIDTH)
    made = pl.pallas_call(
        kernel,
        out_shape=results,
        in_specs=[hbm] * 6 + [vmem] * 2,
        out_specs=(hbm,) * 5,
        scratch_shapes=[
            *[pltpu.VMEM((ROWS, FEATS), BF16)] * 4,
            *[pltpu.VMEM((BLK, FEATS), BF16)] * 2,
            pltpu.VMEM((HEADS, DH, BLK), BF16),
            [[pltpu.VMEM((SPANS + 1, UNIT, WIDTH), BF16)] * NZ] * NC,
            pltpu.VMEM((NC, NZ, PLANE - 1, UNIT, WIDTH), BF16),
            pltpu.VMEM((NC, NZ) + units, BF16),
            pltpu.VMEM((NZ, SPAN, TAB_END), jnp.int32),
            pltpu.SMEM((NZ, SPAN, TAB_END - TAB_S), jnp.int32),
            *[pltpu.VMEM((PAIRS * PAIR_ROWS, FEATS), BF16)] * 2,
            *[pltpu.VMEM((HEADS, BLK, PAIRS * PAIR_ROWS), BF16)] * 2,
            pltpu.VMEM((NC, PAIRS, 2 * HEADS, PAIR_ROWS), F32),
            pltpu.VMEM((NC, 2 * HEADS, ROWS), F32),
            *[pltpu.VMEM((NC, PLANE, NZ, 128), F32)] * 2,
            *[pltpu.VMEM((NC, NZ, PLANE, 128), F32)] * 2,
            pltpu.VMEM((NC, NZ, SPANS, 128), F32),
            *[pltpu.VMEM((NC, PLANE, NZ, 128), F32)] * 2,
            pltpu.VMEM((NC, PAIRS, 2 * HEADS, PAIR_ROWS), F32),
            pltpu.VMEM((NC, 2 * HEADS, ROWS), F32),
            *[pltpu.VMEM((NC, PAIRS) + units, BF16)] * 2,
            *[pltpu.VMEM((NC, 2, 4, ROWS, WIDTH), BF16)] * 2,
            pltpu.VMEM((ROWS, FEATS), F32),
            *[pltpu.VMEM((ROWS, FEATS), BF16)] * 3,
            *[pltpu.VMEM((BLK, FEATS), BF16)] * 2,
            dma((4,)), dma((4,)), dma((7,)),
            dma((NZ,)), dma((NZ,)),
            dma((NC, 2, 4, CHUNKS)), dma((NC, 2, 4, CHUNKS)),
            dma((NC, NZ)), dma((NC, NZ)),
            dma((NC,)), dma((NC,)), dma((NC, NZ)), dma((NC, NZ)),
            dma((NC, NZ)), dma((NC, NZ)), dma((NC,)), dma((NC,)),
            dma((NC, PAIRS)), dma((NC, PAIRS)),
            dma((NC, 2, 4)), dma((NC, 2, 4)),
        ],
        compiler_params=pltpu.CompilerParams(
            collective_id=0, has_side_effects=True, vmem_limit_bytes=60 * 1024 * 1024
        ),
    )(queries, grad_out, new_keys, new_values, cache_keys, cache_values, table, picks)
    return pl.pallas_call(
        hand_over,
        out_shape=results,
        in_specs=[hbm] * 5,
        out_specs=(hbm,) * 5,
        scratch_shapes=[*[pltpu.VMEM(x.shape, BF16) for x in results], dma((2, 5))],
        compiler_params=pltpu.CompilerParams(vmem_limit_bytes=60 * 1024 * 1024),
    )(*made)


def body(queries, new_keys, new_values, grad_out, cache_keys, cache_values, choices):
    z = lax.axis_index("seq") // PLANE
    lanes = jnp.concatenate(
        [
            jnp.arange(256, dtype=jnp.int32) // UNIT,
            jnp.arange(128, dtype=jnp.int32) // NZ,
            jnp.arange(128, dtype=jnp.int32) % PLANE,
        ]
    )
    blocks = jnp.arange(NZ, dtype=jnp.int32)[:, None] * PLANE + lanes[None, :]
    hits = choices[:, :, None, None] == blocks[None, None]
    spans = jnp.arange(SPANS, dtype=jnp.int32)[:, None, None, None]
    table = jnp.min(jnp.where(hits, spans, SPANS), axis=(0, 1))
    table = jnp.broadcast_to(table[:, None, :], (NZ, SPAN, TAB_END))
    away = (choices // PLANE - z) % NZ
    group = jnp.where(away == 0, OWN, jnp.where(away < 4, 2 * away - 1, 14 - 2 * away))
    group = jnp.where(away == 4, FAR, group)
    picks = (group * PLANE + choices % PLANE).T.reshape(TOPK * SPANS, 1)
    picks = jnp.broadcast_to(picks, (TOPK * SPANS, 128))
    return run_kernel(
        queries, grad_out, new_keys, new_values, cache_keys, cache_values, table, picks
    )


def solution(mesh):
    rows = P(("seq", "head"), None)
    both = P("seq", "head")
    return jax.shard_map(
        body,
        mesh=mesh,
        in_specs=(rows, rows, rows, rows, both, both, P("seq", None)),
        out_specs=(both,) * 5,
        check_vma=False,
    )
```

time: 152 us -> 137 us (0.901)
  local copies, waits for them, and re-layouts: 9.84 us -> 2.17 us
  Pallas kernels: 140 us -> 133 us
    unnamed x12 -> x3, local copies, waits for them, and re-layouts: 8.41 us -> 0.74 us
    pallas_call x1 -> x2, Pallas kernels: 140 us -> 133 us  [the longest x1 130 us: run_kernel(): pl.pallas_call(kernel, out_shape=results, in_specs=[hbm] * 6 + [vmem] * 2...]
where the time goes in v3:
time: 137 us; the launch traced here: 136 us
  Pallas kernels  133 us (97%)
  local copies, waits for them, and re-layouts  2.17 us (2%)
    pallas_call x1, Pallas kernels, run_kernel(): pl.pallas_call(kernel, out_shape=results, in_specs=[hbm] * 6 + [vmem] * 2...  130 us
    pallas_call x1, Pallas kernels, run_kernel(): pl.pallas_call(hand_over, out_shape=results, in_specs=[hbm] * 5, out_spec...  2.87 us

profile of v3, /device:TPU:32, one launch (start us, length us, event | category | flops | bytes accessed | tf_op | source)
XLA Modules:
  0.0 136.1 jit_solution(2272720721154649020)
XLA Ops:
  0.7 0.0 copy-start
  0.7 0.7 copy-done
  1.4 0.1 broadcast_in_dim.39
  1.5 0.1 copy.13
  1.6 0.1 broadcast_add_fusion
  1.6 0.2 select_reduce_fusion
  1.8 0.7 broadcast_in_dim.40.sel_ref
  2.5 0.7 broadcast_in_dim.37.tab_ref
  3.1 129.9 %shard_map.110 = (bf16[128,1024]{1,0:T(8,128)(2,1)}, bf16[128,1024]{1,0:T(8,128)(2,1)}, bf16[128,1024]{1,0:T(8,128)(2,1)}, bf16[512,1024]{1,0:T(8,128)(2,1)}, bf16[512,1024]{1,0:T(8,128)(2,1)}) custom-call(bf16[64,2048]{1,0:T(8,128)(2,1)} %q_hbm.1, bf16[64,2048]{1,0:T(8,128)(2,1)} %g_hbm.1, bf16[64,2048]{1,0:T(8,128)(2,1)} %k_hbm.1, bf16[64,2048]{1,0:T(8,128)(2,1)} %v_hbm.1, ...), custom_call_target="tpu_custom_call" | custom-call | tf_op jit(solution)/shard_map/pallas_call | solution.py:603
  133.1 2.9 %shard_map.111 = (bf16[128,1024]{1,0:T(8,128)(2,1)}, bf16[128,1024]{1,0:T(8,128)(2,1)}, bf16[128,1024]{1,0:T(8,128)(2,1)}, bf16[512,1024]{1,0:T(8,128)(2,1)}, bf16[512,1024]{1,0:T(8,128)(2,1)}) custom-call(bf16[128,1024]{1,0:T(8,128)(2,1)} %get-tuple-element.10.refs_0_, bf16[128,1024]{1,0:T(8,128)(2,1)} %get-tuple-element.11.refs_1_, ...), custom_call_target="tpu_custom_call" | custom-call | tf_op jit(solution)/shard_map/pallas_call | solution.py:645
  (5 shorter events, 0.0 us)
Async XLA Ops:
  0.7 0.7 copy-start

commit v4 on v3

--- a/solution.py
+++ b/solution.py
@@ -93,7 +93,7 @@
     q_hbm, g_hbm, k_hbm, v_hbm, ck_hbm, cv_hbm, tab_ref, sel_ref,
     gq_hbm, gnk_hbm, gnv_hbm, gck_hbm, gcv_hbm,
     own_q, own_g, own_k, own_v, kc, vc, kt,
-    zbufs, sbuf, rbuf, tabz, tab_smem, qs, gs, wl, gl,
+    zbufs, sbuf, rbuf, tab_src, tabz, tab_smem, qs, gs, wl, gl,
     stat, own_stat, st_out, st_in, zst_out, zst_in, nz, nr_out, nr_in, joint, own_joint,
     gqb, gr, rs_out, rs_in, own_gq, gq, gnk, gnv, gck, gcv,
     head_send, head_recv, local_sem, tab_send, tab_recv, ring_send, ring_recv,
@@ -158,9 +158,9 @@
     for c in range(NC):
         for i in range(NZ):
             zbufs[c][i][SPANS] = jnp.zeros((UNIT, WIDTH), BF16)
-    stat[...] = jnp.zeros(stat.shape, F32)
-    own_stat[...] = jnp.zeros(own_stat.shape, F32)
-    tabz[OWN] = tab_ref[z]
+    for plane in range(NZ):
+        tab_src[plane] = jnp.broadcast_to(tab_ref[plane:plane + 1, :], (SPAN, TAB_END))
+    tabz[OWN] = tab_src[z]
     pl.semaphore_wait(barrier, 1 + (NZ - 1) + (PLANE - 1))
 
     swaps = [
@@ -172,7 +172,7 @@
     tabs = []
     for d in range(1, NZ):
         i = GROUP_OF[(-d) % NZ]
-        tab = remote(tab_ref.at[(z + d) % NZ], tabz.at[i], tab_send.at[d], tab_recv.at[i], z_peer(d))
+        tab = remote(tab_src.at[(z + d) % NZ], tabz.at[i], tab_send.at[d], tab_recv.at[i], z_peer(d))
         tab.start()
         tabs.append(tab)
     for swap in swaps[2:]:
@@ -217,6 +217,10 @@
         for direction in range(2):
             ring(0, direction, 1, chunk)
 
+    for chunk in range(CHUNKS):
+        lax.fori_loop(2 * chunk, 2 * chunk + 2, pack(1), 0)
+        for direction in range(2):
+            ring(1, direction, 1, chunk)
     for tab in tabs:
         tab.wait_recv()
     to_smem = pltpu.make_async_copy(
@@ -263,8 +267,8 @@
             total = jnp.sum(weights, axis=0, keepdims=True)
             grad_weights = nt(vc[:, cols], gs[pair_rows(p), cols])
             inner = jnp.sum(weights * grad_weights, axis=0, keepdims=True)
-            stat[c, p, pl.ds(k, 1), :] = high + jnp.log(total) * LOG2E
-            stat[c, p, pl.ds(HEADS + k, 1), :] = inner / total
+            stat[p, pl.ds(HALF * c + k, 1), :] = high + jnp.log(total) * LOG2E
+            stat[p, pl.ds(HEADS + HALF * c + k, 1), :] = inner / total
             return carry
 
         lax.fori_loop(0, HALF, one, 0, unroll=HALF)
@@ -283,8 +287,8 @@
             total = jnp.sum(weights, axis=0, keepdims=True)
             grad_weights = nt(own_v[:, cols], own_g[:, cols])
             inner = jnp.sum(weights * grad_weights, axis=0, keepdims=True)
-            own_stat[c, pl.ds(k, 1), :] = high + jnp.log(total) * LOG2E
-            own_stat[c, pl.ds(HEADS + k, 1), :] = inner / total
+            own_stat[pl.ds(HALF * c + k, 1), :] = high + jnp.log(total) * LOG2E
+            own_stat[pl.ds(HEADS + HALF * c + k, 1), :] = inner / total
             return carry
 
         return one
@@ -317,44 +321,41 @@
         lax.fori_loop(1, PLANE, one, 0)
         into[t0] = out[t0]
 
-    small = []
-
-    def stats_plane(c):
-        slots = nt(pick_pair(0), stacked(stat[c, 0]), HIGHEST)
-        for p in range(1, PAIRS):
-            slots += nt(pick_pair(p), stacked(stat[c, p]), HIGHEST)
-        st_out[c] = slots.reshape(PLANE, NZ, 128)
-        plane_all(st_out.at[c], st_in.at[c], st_send.at[c], st_recv.at[c])
-
-    stats_home = {}
-
-    def stats_z(c):
+    def stats_part(p):
+        return nt(pick_pair(p), stacked(stat[p]), HIGHEST)
+
+    def stats_plane(early):
+        st_out[...] = (early + stats_part(3)).reshape(PLANE, NZ, 128)
+        plane_all(st_out, st_in, st_send.at[0], st_recv.at[0])
+
+    stats_home = []
+
+    def stats_z():
         row, lane = iota((128, 128), 0), iota((128, 128), 1)
         swap_order = ((row // PLANE == lane % NZ) & (row % PLANE == lane // NZ)).astype(F32)
-        await_bytes(st_in.at[c, pl.ds(0, PLANE - 1)], st_recv.at[c])
-        zst_out[c] = nn(swap_order, st_in[c].reshape(128, 128), HIGHEST).reshape(NZ, PLANE, 128)
-        stats_home[c] = []
+        await_bytes(st_in.at[pl.ds(0, PLANE - 1)], st_recv.at[0])
+        zst_out[...] = nn(swap_order, st_in[...].reshape(128, 128), HIGHEST).reshape(
+            NZ, PLANE, 128
+        )
         for i in range(NZ):
             j = GROUP_OF[(-OFFSETS[i]) % NZ]
             if i == OWN:
-                zst_in[c, OWN] = zst_out[c, OWN]
                 continue
             copy = remote(
-                zst_out.at[c, i], zst_in.at[c, j], zst_send.at[c, i], zst_recv.at[c, j],
-                z_peer(OFFSETS[i]),
+                zst_out.at[i], zst_in.at[j], zst_send.at[i], zst_recv.at[j], z_peer(OFFSETS[i])
             )
             copy.start()
-            stats_home[c].append(copy)
-            small.append(copy)
-
-    norms_out = {}
-
-    def norms_z(c):
-        own_slots = nt(pick_own(), stacked(own_stat[c]), HIGHEST)
+            stats_home.append(copy)
+        zst_in[OWN] = zst_out[OWN]
+
+    norms_out = []
+
+    def norms_z():
+        own_slots = nt(pick_own(), stacked(own_stat[...]), HIGHEST)
         chosen = (sel_ref[...] == iota((TOPK * SPANS, 128), 1)).astype(F32)
-        for copy in stats_home[c]:
+        for copy in stats_home:
             copy.wait_recv()
-        picked = nn(chosen, zst_in[c].reshape(128, 128), HIGHEST)
+        picked = nn(chosen, zst_in[...].reshape(128, 128), HIGHEST)
         logs = [own_slots] + [picked[SPANS * t:SPANS * (t + 1)] for t in range(TOPK)]
         peak = jnp.maximum(jnp.maximum(logs[0], logs[1]), jnp.maximum(logs[2], logs[3]))
         shares = [jnp.exp2(log - peak) for log in logs]
@@ -364,19 +365,15 @@
         for share, log in zip(shares, logs):
             delta += pltpu.roll(share / total, HEADS, 1) * log
         is_norm = iota((SPANS, 128), 1) % (2 * HEADS) < HEADS
-        nz[c, OWN] = jnp.where(is_norm, norm, delta)
-        norms_out[c] = []
+        nz[OWN] = jnp.where(is_norm, norm, delta)
         for d in range(1, NZ):
             i = GROUP_OF[(-d) % NZ]
-            copy = remote(
-                nz.at[c, OWN], nz.at[c, i], nz_send.at[c, d], nz_recv.at[c, i], z_peer(d)
-            )
+            copy = remote(nz.at[OWN], nz.at[i], nz_send.at[d], nz_recv.at[i], z_peer(d))
             copy.start()
-            norms_out[c].append(copy)
-            small.append(copy)
-        own_joint[c] = unstacked(tn(nz[c, OWN], pick_own(), HIGHEST))
-
-    def norms_plane(c):
+            norms_out.append(copy)
+        own_joint[...] = unstacked(tn(nz[OWN], pick_own(), HIGHEST))
+
+    def norms_plane():
         lane8 = iota((SPANS, 128), 1) % NZ
         span_row = iota((SPANS, 128), 0)
         routes = jnp.concatenate(
@@ -386,21 +383,17 @@
             ],
             axis=0,
         ).astype(F32)
-        for copy in norms_out[c]:
+        for copy in norms_out:
             copy.wait_recv()
-        routed = tn(routes, nz[c].reshape(128, 128), HIGHEST)
-        nr_out[c] = routed.reshape(PLANE, NZ, 128)
-        plane_all(nr_out.at[c], nr_in.at[c], nr_send.at[c], nr_recv.at[c])
-
-    def norms_arrived(c):
-        await_bytes(nr_in.at[c, pl.ds(0, PLANE - 1)], nr_recv.at[c])
+        nr_out[...] = tn(routes, nz[...].reshape(128, 128), HIGHEST).reshape(PLANE, NZ, 128)
+        plane_all(nr_out, nr_in, nr_send.at[0], nr_recv.at[0])
 
     def own_second(c):
         def one(k, carry):
             cols = head_cols(HALF * c + k)
-            weights = jnp.exp2(own_scores(cols) - own_joint[c, pl.ds(k, 1), :])
+            weights = jnp.exp2(own_scores(cols) - own_joint[pl.ds(HALF * c + k, 1), :])
             grad_weights = nt(own_v[:, cols], own_g[:, cols])
-            grad_scores = weights * (grad_weights - own_joint[c, pl.ds(HEADS + k, 1), :])
+            grad_scores = weights * (grad_weights - own_joint[pl.ds(HEADS + HALF * c + k, 1), :])
             weights_low = weights.astype(BF16)
             grad_low = grad_scores.astype(BF16)
             own_gq[:, cols] = tn(grad_low, own_k[:, cols]) * SCALING
@@ -411,15 +404,16 @@
         lax.fori_loop(0, HALF, one, 0, unroll=2)
 
     def second(c, p):
-        joint[c, p] = unstacked(tn(nr_in[c].reshape(128, 128), pick_pair(p), HIGHEST))
+        if c == 0:
+            joint[p] = unstacked(tn(nr_in[...].reshape(128, 128), pick_pair(p), HIGHEST))
 
         def one(k, carry):
             h = HALF * c + k
             cols = head_cols(h)
             scores = nt(kc[:, cols], qs[pair_rows(p), cols]) * SCALING2
-            weights = jnp.exp2(scores - joint[c, p, pl.ds(k, 1), :])
+            weights = jnp.exp2(scores - joint[p, pl.ds(h, 1), :])
             grad_weights = nt(vc[:, cols], gs[pair_rows(p), cols])
-            grad_scores = weights * (grad_weights - joint[c, p, pl.ds(HEADS + k, 1), :])
+            grad_scores = weights * (grad_weights - joint[p, pl.ds(HEADS + h, 1), :])
             grad_low = grad_scores.astype(BF16)
             wl[h, :, pair_rows(p)] = weights.astype(BF16)
             gl[h, :, pair_rows(p)] = grad_low
@@ -501,80 +495,76 @@
             ring(1, direction, 1, chunk)
 
     spread(0, OWN)
+    spread(1, OWN)
     for i in (2, 3):
         keeps[i].wait()
         swaps[i].wait_recv()
     fetch_k.wait()
     fetch_v.wait()
     ring_step(0, 1, own_work)
-    ring_step(0, 2, turn_work)
-    ring_step(0, 3, next_half)
-    spread(1, OWN)
+    ring_step(1, 1, turn_work)
+    ring_step(0, 2, nothing)
+    ring_step(1, 2, nothing)
+    first(0, 0)
+    ring_step(0, 3, nothing)
+    first(1, 0)
+    ring_step(1, 3, nothing)
+    first(0, 1)
     ring_step(0, 4, nothing)
-    first(0, 0)
-    ring_step(1, 1, nothing)
-    first(0, 1)
-    ring_step(1, 2, nothing)
+    first(1, 1)
+    ring_step(1, 4, nothing)
     first(0, 2)
+    first(1, 2)
     first(0, 3)
-    stats_plane(0)
-    ring_step(1, 3, nothing)
-    stats_z(0)
-    ring_step(1, 4, nothing)
-    norms_z(0)
-    first(1, 0)
-    first(1, 1)
-    norms_plane(0)
-    first(1, 2)
+    early = stats_part(0) + stats_part(1) + stats_part(2)
     first(1, 3)
-    stats_plane(1)
-    norms_arrived(0)
-    second(0, 3)
-    second(0, 2)
-    stats_z(1)
-    second(0, 1)
-    second(0, 0)
-    norms_z(1)
-    home(0, 1)
+    stats_plane(early)
+    stats_z()
+    norms_z()
     own_second(0)
-    norms_plane(1)
-    home(0, 2)
-    norms_arrived(1)
-    second(1, 3)
-    second(1, 2)
-    home(0, 3)
-    second(1, 1)
-    second(1, 0)
-    home(0, 4)
+    norms_plane()
     own_second(1)
     store_nk = pltpu.make_async_copy(gnk, gnk_hbm, local_sem.at[0])
     store_nv = pltpu.make_async_copy(gnv, gnv_hbm, local_sem.at[1])
     store_nk.start()
     store_nv.start()
+    await_bytes(nr_in.at[pl.ds(0, PLANE - 1)], nr_recv.at[0])
+    second(0, 3)
+    second(1, 3)
+    second(0, 2)
+    second(1, 2)
+    home(0, 1)
+    second(0, 1)
     home(1, 1)
+    second(1, 1)
+    home(0, 2)
+    second(0, 0)
+    home(1, 2)
+    second(1, 0)
     cache_grads(0)
-    home(1, 2)
     cache_grads(1)
     store_k = pltpu.make_async_copy(gck, gck_hbm, local_sem.at[5])
     store_v = pltpu.make_async_copy(gcv, gcv_hbm, local_sem.at[6])
     store_k.start()
     store_v.start()
+    home(0, 3)
     home(1, 3)
+    home(0, 4)
     home(1, 4)
     finish(0)
     finish(1)
     store_q = pltpu.make_async_copy(gq, gq_hbm, local_sem.at[2])
     store_q.start()
 
-    for copy in swaps + tabs + small + list(rings.values()) + list(homes.values()):
+    for copy in swaps + tabs + stats_home + norms_out + list(rings.values()) + list(homes.values()):
         copy.wait_send()
     for c in range(NC):
         for i in range(NZ):
             await_bytes(sbuf.at[c, i], plane_send.at[c, i])
-        await_bytes(st_out.at[c, pl.ds(0, PLANE - 1)], st_send.at[c])
-        await_bytes(nr_out.at[c, pl.ds(0, PLANE - 1)], nr_send.at[c])
         for p in range(PAIRS):
             await_bytes(gqb.at[c, p, pl.ds(0, PLANE - 1)], gr_send.at[c, p])
+    await_bytes(st_out.at[pl.ds(0, PLANE - 1)], st_send.at[0])
+    await_bytes(nr_out.at[pl.ds(0, PLANE - 1)], nr_send.at[0])
     for store in (store_nk, store_nv, store_k, store_v, store_q):
         store.wait()
 
@@ -612,18 +602,18 @@
             [[pltpu.VMEM((SPANS + 1, UNIT, WIDTH), BF16)] * NZ] * NC,
             pltpu.VMEM((NC, NZ, PLANE - 1, UNIT, WIDTH), BF16),
             pltpu.VMEM((NC, NZ) + units, BF16),
-            pltpu.VMEM((NZ, SPAN, TAB_END), jnp.int32),
+            *[pltpu.VMEM((NZ, SPAN, TAB_END), jnp.int32)] * 2,
             pltpu.SMEM((NZ, SPAN, TAB_END - TAB_S), jnp.int32),
             *[pltpu.VMEM((PAIRS * PAIR_ROWS, FEATS), BF16)] * 2,
             *[pltpu.VMEM((HEADS, BLK, PAIRS * PAIR_ROWS), BF16)] * 2,
-            pltpu.VMEM((NC, PAIRS, 2 * HEADS, PAIR_ROWS), F32),
-            pltpu.VMEM((NC, 2 * HEADS, ROWS), F32),
-            *[pltpu.VMEM((NC, PLANE, NZ, 128), F32)] * 2,
-            *[pltpu.VMEM((NC, NZ, PLANE, 128), F32)] * 2,
-            pltpu.VMEM((NC, NZ, SPANS, 128), F32),
-            *[pltpu.VMEM((NC, PLANE, NZ, 128), F32)] * 2,
-            pltpu.VMEM((NC, PAIRS, 2 * HEADS, PAIR_ROWS), F32),
-            pltpu.VMEM((NC, 2 * HEADS, ROWS), F32),
+            pltpu.VMEM((PAIRS, 2 * HEADS, PAIR_ROWS), F32),
+            pltpu.VMEM((2 * HEADS, ROWS), F32),
+            *[pltpu.VMEM((PLANE, NZ, 128), F32)] * 2,
+            *[pltpu.VMEM((NZ, PLANE, 128), F32)] * 2,
+            pltpu.VMEM((NZ, SPANS, 128), F32),
+            *[pltpu.VMEM((PLANE, NZ, 128), F32)] * 2,
+            pltpu.VMEM((PAIRS, 2 * HEADS, PAIR_ROWS), F32),
+            pltpu.VMEM((2 * HEADS, ROWS), F32),
             *[pltpu.VMEM((NC, PAIRS) + units, BF16)] * 2,
             *[pltpu.VMEM((NC, 2, 4, ROWS, WIDTH), BF16)] * 2,
             pltpu.VMEM((ROWS, FEATS), F32),
@@ -633,8 +623,8 @@
             dma((NZ,)), dma((NZ,)),
             dma((NC, 2, 4, CHUNKS)), dma((NC, 2, 4, CHUNKS)),
             dma((NC, NZ)), dma((NC, NZ)),
-            dma((NC,)), dma((NC,)), dma((NC, NZ)), dma((NC, NZ)),
-            dma((NC, NZ)), dma((NC, NZ)), dma((NC,)), dma((NC,)),
+            dma((1,)), dma((1,)), dma((NZ,)), dma((NZ,)),
+            dma((NZ,)), dma((NZ,)), dma((1,)), dma((1,)),
             dma((NC, PAIRS)), dma((NC, PAIRS)),
             dma((NC, 2, 4)), dma((NC, 2, 4)),
         ],
@@ -665,12 +655,10 @@
     hits = choices[:, :, None, None] == blocks[None, None]
     spans = jnp.arange(SPANS, dtype=jnp.int32)[:, None, None, None]
     table = jnp.min(jnp.where(hits, spans, SPANS), axis=(0, 1))
-    table = jnp.broadcast_to(table[:, None, :], (NZ, SPAN, TAB_END))
     away = (choices // PLANE - z) % NZ
     group = jnp.where(away == 0, OWN, jnp.where(away < 4, 2 * away - 1, 14 - 2 * away))
     group = jnp.where(away == 4, FAR, group)
     picks = (group * PLANE + choices % PLANE).T.reshape(TOPK * SPANS, 1)
-    picks = jnp.broadcast_to(picks, (TOPK * SPANS, 128))
     return run_kernel(
         queries, grad_out, new_keys, new_values, cache_keys, cache_values, table, picks
     )

time: 137 us -> 132 us (0.964)
  Pallas kernels: 133 us -> 127 us
    pallas_call x1, Pallas kernels: 130 us -> 124 us  [run_kernel(): pl.pallas_call(kernel, out_shape=results, in_specs=[hbm] * 6 + [vmem] * 2...]
    broadcast_in_dim x3 -> x0, local copies, waits for them, and re-layouts: 1.43 us -> none  [the longest x2 0.77 us: body(): picks = jnp.broadcast_to(picks, (TOPK * SPANS, 128))]
where the time goes in v4:
time: 132 us; the launch traced here: 131 us
  Pallas kernels  127 us (96%)
  local copies, waits for them, and re-layouts  1.44 us (1%)
    pallas_call x1, Pallas kernels, run_kernel(): pl.pallas_call(kernel, out_shape=results, in_specs=[hbm] * 6 + [vmem] * 2...  124 us
    pallas_call x1, Pallas kernels, run_kernel(): pl.pallas_call(hand_over, out_shape=results, in_specs=[hbm] * 5, out_spec...  2.87 us

profile of v4, /device:TPU:32, one launch (start us, length us, event | category | flops | bytes accessed | tf_op | source)
XLA Modules:
  0.0 130.5 jit_solution(12219987472464212575)
XLA Ops:
  0.7 0.0 copy-start
  0.7 0.7 copy-done
  1.4 0.1 copy.14
  1.5 0.1 broadcast_add_fusion
  1.5 0.8 select_reduce_fusion.tab_ref
  2.3 0.7 reshape.48.sel_ref
  3.0 124.4 %shard_map.110 = (bf16[128,1024]{1,0:T(8,128)(2,1)}, bf16[128,1024]{1,0:T(8,128)(2,1)}, bf16[128,1024]{1,0:T(8,128)(2,1)}, bf16[512,1024]{1,0:T(8,128)(2,1)}, bf16[512,1024]{1,0:T(8,128)(2,1)}) custom-call(bf16[64,2048]{1,0:T(8,128)(2,1)} %q_hbm.1, bf16[64,2048]{1,0:T(8,128)(2,1)} %g_hbm.1, bf16[64,2048]{1,0:T(8,128)(2,1)} %k_hbm.1, bf16[64,2048]{1,0:T(8,128)(2,1)} %v_hbm.1, ...), custom_call_target="tpu_custom_call" | custom-call | tf_op jit(solution)/shard_map/pallas_call | solution.py:593
  127.5 2.9 %shard_map.111 = (bf16[128,1024]{1,0:T(8,128)(2,1)}, bf16[128,1024]{1,0:T(8,128)(2,1)}, bf16[128,1024]{1,0:T(8,128)(2,1)}, bf16[512,1024]{1,0:T(8,128)(2,1)}, bf16[512,1024]{1,0:T(8,128)(2,1)}) custom-call(bf16[128,1024]{1,0:T(8,128)(2,1)} %get-tuple-element.10.refs_0_, bf16[128,1024]{1,0:T(8,128)(2,1)} %get-tuple-element.11.refs_1_, ...), custom_call_target="tpu_custom_call" | custom-call | tf_op jit(solution)/shard_map/pallas_call | solution.py:635
  (5 shorter events, 0.0 us)
Async XLA Ops:
  0.7 0.7 copy-start

commit v5 on v4

--- a/solution.py
+++ b/solution.py
@@ -154,7 +154,7 @@
         )
         return carry
 
-    lax.fori_loop(1, PLANE, greet, 0)
+    lax.fori_loop(1, PLANE, greet, 0, unroll=PLANE - 1)
     for c in range(NC):
         for i in range(NZ):
             zbufs[c][i][SPANS] = jnp.zeros((UNIT, WIDTH), BF16)
@@ -239,7 +239,7 @@
             ).start()
             return carry
 
-        lax.fori_loop(1, PLANE, one, 0)
+        lax.fori_loop(1, PLANE, one, 0, unroll=PLANE - 1)
         rbuf[c, i, t0] = zbufs[c][i][tab_smem[i, 0, t0]]
 
     def pair_rows(p):
@@ -257,7 +257,7 @@
             gs[rows, half_cols(c)] = jnp.concatenate([a[SPAN:], b[SPAN:]], axis=0).astype(BF16)
             return carry
 
-        lax.fori_loop(0, PLANE, unpack, 0)
+        lax.fori_loop(0, PLANE, unpack, 0, unroll=4)
 
         def one(k, carry):
             cols = head_cols(HALF * c + k)
@@ -318,7 +318,7 @@
             remote(out.at[t], into.at[t0], send, recv, plane_peer(t)).start()
             return carry
 
-        lax.fori_loop(1, PLANE, one, 0)
+        lax.fori_loop(1, PLANE, one, 0, unroll=PLANE - 1)
         into[t0] = out[t0]
 
     def stats_part(p):

time: 132 us -> 130 us (0.985)
  no operation moved by 1% of the time
where the time goes in v5:
time: 130 us; the launch traced here: 129 us
  Pallas kernels  126 us (97%)
  local copies, waits for them, and re-layouts  1.44 us (1%)
    pallas_call x1, Pallas kernels, run_kernel(): pl.pallas_call(kernel, out_shape=results, in_specs=[hbm] * 6 + [vmem] * 2...  123 us
    pallas_call x1, Pallas kernels, run_kernel(): pl.pallas_call(hand_over, out_shape=results, in_specs=[hbm] * 5, out_spec...  2.87 us

profile of v5, /device:TPU:32, one launch (start us, length us, event | category | flops | bytes accessed | tf_op | source)
XLA Modules:
  0.0 129.3 jit_solution(13667848091396399308)
XLA Ops:
  0.7 0.0 copy-start
  0.7 0.7 copy-done
  1.4 0.1 copy.14
  1.5 0.1 broadcast_add_fusion
  1.5 0.8 select_reduce_fusion.tab_ref
  2.3 0.7 reshape.48.sel_ref
  3.0 123.2 %shard_map.110 = (bf16[128,1024]{1,0:T(8,128)(2,1)}, bf16[128,1024]{1,0:T(8,128)(2,1)}, bf16[128,1024]{1,0:T(8,128)(2,1)}, bf16[512,1024]{1,0:T(8,128)(2,1)}, bf16[512,1024]{1,0:T(8,128)(2,1)}) custom-call(bf16[64,2048]{1,0:T(8,128)(2,1)} %q_hbm.1, bf16[64,2048]{1,0:T(8,128)(2,1)} %g_hbm.1, bf16[64,2048]{1,0:T(8,128)(2,1)} %k_hbm.1, bf16[64,2048]{1,0:T(8,128)(2,1)} %v_hbm.1, ...), custom_call_target="tpu_custom_call" | custom-call | tf_op jit(solution)/shard_map/pallas_call | solution.py:593
  126.2 2.9 %shard_map.111 = (bf16[128,1024]{1,0:T(8,128)(2,1)}, bf16[128,1024]{1,0:T(8,128)(2,1)}, bf16[128,1024]{1,0:T(8,128)(2,1)}, bf16[512,1024]{1,0:T(8,128)(2,1)}, bf16[512,1024]{1,0:T(8,128)(2,1)}) custom-call(bf16[128,1024]{1,0:T(8,128)(2,1)} %get-tuple-element.10.refs_0_, bf16[128,1024]{1,0:T(8,128)(2,1)} %get-tuple-element.11.refs_1_, ...), custom_call_target="tpu_custom_call" | custom-call | tf_op jit(solution)/shard_map/pallas_call | solution.py:635
  (5 shorter events, 0.0 us)
Async XLA Ops:
  0.7 0.7 copy-start
